TPU v7x, 32 devices: a whole 2x2x4 slice. The times are simulated.
32 devices in a mesh: groups: 2 (over y), seq: 4 (over z), head: 4 (over x, core).
Axes of the slice: x: 2, y: 2, z: 4, core: 2. Of those that a mesh axis runs over, the one named last changes fastest.
Arguments:
- hidden: bfloat16 [2048, 2560], P(('groups', 'seq'), 'head'), parts along dimension 0, may hold values from -6 to 6
- w_zx: bfloat16 [2560, 2, 3072], P('seq', None, 'head'), may hold values from -0.125 to 0.125
- w_dt: bfloat16 [2560, 48], P('seq', 'head'), may hold values from -0.125 to 0.125
- w_bc: bfloat16 [2560, 2, 128], P('seq'), may hold values from -0.125 to 0.125
- dt_bias: float32 [48], P('head'), may hold values from -1 to 0
- a_log: float32 [48], P('head'), may hold values from -12 to -2, as said below
- d_skip: float32 [48], P('head'), may hold values from 0.5 to 1.5
- norm_gain: float32 [3072], P('head'), may hold values from 0.5 to 1.5
- w_out: bfloat16 [3072, 2560], P('head', 'seq'), may hold values from -0.109375 to 0.109375
- grad_out: bfloat16 [2048, 2560], P(('groups', 'seq'), 'head'), parts along dimension 0, may hold values from -6 to 6
Outputs:
- layer_out: bfloat16 [2048, 2560], P(('groups', 'seq'), 'head'), parts along dimension 0
- grad_hidden: bfloat16 [2048, 2560], P(('groups', 'seq'), 'head'), parts along dimension 0
- grad_wzx: float32 [5120, 2, 3072], P(('groups', 'seq'), None, 'head'), parts along dimension 0
- grad_wdt: float32 [5120, 48], P(('groups', 'seq'), 'head'), parts along dimension 0
- grad_wbc: float32 [5120, 2, 128], P(('groups', 'seq')), parts along dimension 0
- grad_dtbias: float32 [96], P(('groups', 'head')), parts along dimension 0
- grad_alog: float32 [96], P(('groups', 'head')), parts along dimension 0
- grad_dskip: float32 [96], P(('groups', 'head')), parts along dimension 0
- grad_gain: float32 [6144], P(('groups', 'head')), parts along dimension 0
- grad_wout: float32 [6144, 2560], P(('groups', 'head'), 'seq'), parts along dimension 0
There are 2 independent parts, one for each index of `groups`. A program takes and returns all parts, laid end to end along the dimension named above; an argument that names none is the same for every part. Nothing has to cross between parts.
Inputs may be any that keep to these rules, and one draw needn't show every extreme that they name: `a_log`: log of each head's decay rate.
All inputs are finite; a program needn't handle non-finite values.
Results may differ from a plain program's by a relative error of at most 0.029.
Values may be sent and summed in bfloat16 or wider, within the bound.
A program may use at most 128 MiB of HBM per device.

v0:
```python
import jax
import jax.numpy as jnp
from jax import lax
from jax.sharding import PartitionSpec as P

HEADS = 48
HDIM = 64
BLOCK = 128


EPS_NORM = 1e-05
HIGH = lax.Precision.HIGHEST


def entering(x, axis, combine, identity):
    peers, here = (lax.axis_size(axis), lax.axis_index(axis))
    everything = jax.tree.map(
        lambda part, kind: lax.all_gather(part.astype(kind), axis), x, (jnp.bfloat16, jnp.bfloat16)
    )
    start = jax.tree.map(
        lambda part, zero: jnp.broadcast_to(jnp.asarray(zero, part.dtype), part.shape), x, identity
    )

    def entering_lap(k, before):
        reached = k < here
        new = combine(
            before, jax.tree.map(lambda part, own: part[k].astype(own.dtype), everything, x)
        )
        return jax.tree.map(lambda a, b: jnp.where(reached, a, b), new, before)

    return lax.fori_loop(0, peers, entering_lap, start)


def carried_in(x, axis, combine, identity):
    peers, here = (lax.axis_size(axis), lax.axis_index(axis))
    everything = jax.tree.map(
        lambda part, kind: lax.all_gather(part.astype(kind), axis),
        x,
        jax.tree.map(lambda a: jnp.bfloat16 if a.dtype == jnp.float32 else a.dtype, x),
    )
    start = jax.tree.map(
        lambda part, zero: jnp.broadcast_to(jnp.asarray(zero, part.dtype), part.shape), x, identity
    )

    def carried_lap(k, before):
        at = peers - 1 - k
        reached = at > here
        new = combine(
            before, jax.tree.map(lambda part, own: part[at].astype(own.dtype), everything, x)
        )
        return jax.tree.map(lambda a, b: jnp.where(reached, a, b), new, before)

    return lax.fori_loop(0, peers, carried_lap, start)


def split_inputs(zx_f, dtr_f, bc_f, dt_bias, a_log):
    rows = dtr_f.shape[0]
    nheads = dtr_f.shape[1]
    width = zx_f.shape[2] // nheads
    z_gate = zx_f[:, 0]
    x_in = jax.nn.silu(zx_f[:, 1]).reshape(rows, nheads, width)
    dt_val = jax.nn.softplus(dtr_f + dt_bias[None])
    log_decay = -dt_val * jnp.exp(a_log)[None]
    return (z_gate, x_in, dt_val, log_decay, bc_f[:, 0], bc_f[:, 1])


def ssd_pass(x_in, dt_val, log_decay, b_in, c_in, d_skip, s_init, with_out):
    rows, nheads, width = x_in.shape
    blocks = rows // BLOCK
    lower = jnp.arange(BLOCK)[:, None] >= jnp.arange(BLOCK)[None, :]
    parts = (
        x_in.reshape(blocks, BLOCK, nheads, width),
        dt_val.reshape(blocks, BLOCK, nheads),
        log_decay.reshape(blocks, BLOCK, nheads),
        b_in.reshape(blocks, BLOCK, -1),
        c_in.reshape(blocks, BLOCK, -1),
    )

    def advance(state, block):
        x_blk, dt_blk, ld_blk, b_blk, c_blk = block
        cumul = jnp.cumsum(ld_blk, axis=0)
        tail = cumul[-1]
        inflow = jnp.exp(tail[None] - cumul) * dt_blk
        fresh = state * jnp.exp(tail)[:, None, None] + jnp.einsum(
            "sh,shp,sn->hpn", inflow, x_blk, b_blk, precision=HIGH
        )
        if not with_out:
            return (fresh, None)
        scores = jnp.dot(c_blk, b_blk.T, precision=HIGH)
        gaps = cumul.T[:, :, None] - cumul.T[:, None, :]
        weights = jnp.exp(jnp.where(lower[None], gaps, -1e30)) * scores[None] * dt_blk.T[:, None, :]
        y_blk = jnp.einsum("hts,shp->thp", weights, x_blk, precision=HIGH)
        y_blk = (
            y_blk
            + jnp.einsum("tn,hpn->thp", c_blk, state, precision=HIGH) * jnp.exp(cumul)[:, :, None]
        )
        y_blk = y_blk + d_skip[None, :, None] * x_blk
        return (fresh, y_blk)

    final, outs = lax.scan(advance, s_init, parts)
    return (outs, final)


def mixer(zx_f, dtr_f, bc_f, dt_bias, a_log, d_skip, s_init):
    z_gate, x_in, dt_val, log_decay, b_in, c_in = split_inputs(zx_f, dtr_f, bc_f, dt_bias, a_log)
    outs, final = ssd_pass(x_in, dt_val, log_decay, b_in, c_in, d_skip, s_init, True)
    return outs.reshape(z_gate.shape[0], -1) * jax.nn.silu(z_gate)


def local_states(zx_f, dtr_f, bc_f, dt_bias, a_log):
    z_gate, x_in, dt_val, log_decay, b_in, c_in = split_inputs(zx_f, dtr_f, bc_f, dt_bias, a_log)
    start_state = jnp.zeros((x_in.shape[1], x_in.shape[2], b_in.shape[1]), x_in.dtype)
    outs, final = ssd_pass(x_in, dt_val, log_decay, b_in, c_in, None, start_state, False)
    return (final, jnp.sum(log_decay, axis=0))


def combine(earlier, later):
    return (earlier[0] * later[0], later[0][:, None, None] * earlier[1] + later[1])


def split_pair(value):
    upper = value.astype(jnp.bfloat16)
    lower_part = (value - upper.astype(value.dtype)).astype(jnp.bfloat16)
    return (upper, lower_part)


def input_rows_term(grads, pieces):
    count = pieces[0].shape[0]
    term = jnp.einsum(
        "tc,dc->td", grads[0], pieces[0].reshape(count, -1), preferred_element_type=jnp.float32
    )
    term = term + jnp.einsum("th,dh->td", grads[1], pieces[1], preferred_element_type=jnp.float32)
    flat_bc = pieces[2].reshape(count, -1)
    term = term + jnp.einsum("tc,dc->td", grads[2], flat_bc, preferred_element_type=jnp.float32)
    return term + jnp.einsum("tc,dc->td", grads[3], flat_bc, preferred_element_type=jnp.float32)


def on_device(hidden, w_zx, w_dt, w_bc, dt_bias, a_log, d_skip, norm_gain, w_out, grad_out):
    tokens = hidden.shape[0]
    wide = HEADS * HDIM
    local_cols = w_zx.shape[1] * w_zx.shape[2]
    bc_cols = w_bc.shape[1] * w_bc.shape[2]
    head_cols = w_dt.shape[1]
    full_in = lax.all_gather(hidden, "head", axis=1, tiled=True)
    pieces = (
        lax.all_gather(w_zx, "seq", axis=0, tiled=True),
        lax.all_gather(w_dt, "seq", axis=0, tiled=True),
        lax.all_gather(w_bc, "seq", axis=0, tiled=True),
    )
    count = pieces[0].shape[0]
    cols = full_in
    zx_acc = jnp.dot(cols, pieces[0].reshape(count, local_cols), preferred_element_type=jnp.float32)
    dt_acc = jnp.dot(cols, pieces[1], preferred_element_type=jnp.float32)
    bc_acc = jnp.dot(cols, pieces[2].reshape(count, bc_cols), preferred_element_type=jnp.float32)
    zx_b, dtr_b, bc_b = lax.optimization_barrier(
        (zx_acc.astype(jnp.bfloat16), dt_acc.astype(jnp.bfloat16), bc_acc.astype(jnp.bfloat16))
    )
    zx_f = zx_b.astype(jnp.float32).reshape(tokens, 2, -1)
    dtr_f = dtr_b.astype(jnp.float32)
    bc_f = bc_b.astype(jnp.float32).reshape(tokens, 2, -1)
    (s_local, log_total), pull_states = jax.vjp(local_states, zx_f, dtr_f, bc_f, dt_bias, a_log)
    decay = jnp.exp(log_total)
    identity = (jnp.ones_like(decay), jnp.zeros_like(s_local))
    s_in = entering((decay, s_local), "seq", combine, identity)[1]
    mixed, pull_mixer = jax.vjp(mixer, zx_f, dtr_f, bc_f, dt_bias, a_log, d_skip, s_in)
    squares = lax.psum(jnp.sum(mixed * mixed, axis=1), "head")
    rinv = lax.rsqrt(squares / wide + EPS_NORM)
    gated = (mixed * rinv[:, None] * norm_gain[None]).astype(jnp.bfloat16)
    partial_value = jnp.dot(
        gated, lax.all_gather(w_out, "seq", axis=1, tiled=True), preferred_element_type=jnp.float32
    )
    layer_out = lax.psum_scatter(
        partial_value.astype(jnp.bfloat16), "head", scatter_dimension=1, tiled=True
    )
    full_grad = lax.all_gather(grad_out, "head", axis=1, tiled=True)
    piece = lax.all_gather(w_out, "seq", axis=1, tiled=True)
    cols = full_grad
    back = jnp.einsum("tr,kr->tk", cols, piece, preferred_element_type=jnp.float32)
    grad_gated = lax.optimization_barrier(back.astype(jnp.bfloat16))
    out_term = jnp.einsum("tk,td->kd", gated, full_grad, preferred_element_type=jnp.float32)
    grad_wout = lax.psum_scatter(
        out_term.astype(jnp.bfloat16), "seq", scatter_dimension=1, tiled=True
    ).astype(jnp.float32)
    upstream = grad_gated.astype(jnp.float32)
    gain_part = jnp.sum(upstream * mixed * rinv[:, None], axis=0)
    inner = lax.psum(jnp.sum(upstream * norm_gain[None] * mixed, axis=1), "head")
    grad_mixed = (
        rinv[:, None] * norm_gain[None] * upstream
        - mixed * (rinv * rinv * rinv * inner / wide)[:, None]
    )
    first = pull_mixer(grad_mixed)
    ds_in = first[6]
    carried = carried_in((decay, ds_in), "seq", combine, identity)[1]
    grad_log = decay * jnp.sum(carried * s_in, axis=(1, 2))
    second = pull_states((carried, grad_log))
    d_zx = (first[0] + second[0]).reshape(tokens, -1).astype(jnp.bfloat16)
    d_dtr = (first[1] + second[1]).astype(jnp.bfloat16)
    d_bc = (first[2] + second[2]).reshape(tokens, -1)
    bc_upper, bc_lower = split_pair(d_bc)
    grad_dtbias, grad_alog, grad_dskip, grad_gain = lax.psum(
        (first[3] + second[3], first[4] + second[4], first[5], gain_part), "seq"
    )
    term = input_rows_term(
        (d_zx, d_dtr, bc_upper, bc_lower),
        lax.all_gather((w_zx, w_dt, w_bc), "seq", axis=0, tiled=True),
    )
    grad_hidden = lax.psum_scatter(
        term.astype(jnp.bfloat16), "head", scatter_dimension=1, tiled=True
    )
    bc_total = lax.psum(d_bc.astype(jnp.bfloat16), "head").astype(jnp.float32)
    total_upper, total_lower = split_pair(bc_total)
    cols = full_in
    bc_term = jnp.einsum(
        "tr,tc->rc", cols, total_upper, preferred_element_type=jnp.float32
    ) + jnp.einsum("tr,tc->rc", cols, total_lower, preferred_element_type=jnp.float32)
    sums = lax.psum_scatter(
        jnp.concatenate(
            [
                jnp.einsum("tr,tc->rc", cols, d_zx, preferred_element_type=jnp.float32),
                jnp.einsum("tr,th->rh", cols, d_dtr, preferred_element_type=jnp.float32),
                bc_term,
            ],
            axis=1,
        ).astype(jnp.bfloat16),
        "seq",
        scatter_dimension=0,
        tiled=True,
    ).astype(jnp.float32)
    rows_here = w_zx.shape[0]
    grad_wzx = sums[:, :local_cols].reshape(rows_here, 2, -1)
    grad_wdt = sums[:, local_cols : local_cols + head_cols]
    grad_wbc = sums[:, local_cols + head_cols :].reshape(rows_here, 2, -1)
    return (
        layer_out,
        grad_hidden,
        grad_wzx,
        grad_wdt,
        grad_wbc,
        grad_dtbias,
        grad_alog,
        grad_dskip,
        grad_gain,
        grad_wout,
    )


def solution(mesh):
    in_specs = (
        P(("groups", "seq"), "head"),
        P("seq", None, "head"),
        P("seq", "head"),
        P("seq", None, None),
        P("head"),
        P("head"),
        P("head"),
        P("head"),
        P("head", "seq"),
        P(("groups", "seq"), "head"),
    )
    out_specs = (
        P(("groups", "seq"), "head"),
        P(("groups", "seq"), "head"),
        P(("groups", "seq"), None, "head"),
        P(("groups", "seq"), "head"),
        P(("groups", "seq"), None, None),
        P(("groups", "head")),
        P(("groups", "head")),
        P(("groups", "head")),
        P(("groups", "head")),
        P(("groups", "head"), "seq"),
    )
    return jax.shard_map(
        on_device, mesh=mesh, in_specs=in_specs, out_specs=out_specs, check_vma=False
    )
```

profile of v0, /device:TPU:2, one launch (start us, length us, event | category | flops | bytes accessed | tf_op | source)
XLA Modules:
  0.0 990.5 jit_solution(12451117494271212644)
XLA Ops:
  7.2 1.9 copy.203
  14.7 14.0 %all_gather.42 = bf16[2560,12]{0,1:T(8,128)(2,1)S(1)} all-gather(bf16[640,12]{0,1:T(8,128)(2,1)S(1)} %copy-done.63), channel_id=1, replica_groups=mesh['groups'=2,'seq'=4,'head'=4] {'seq'}, dimensions={0}, use_global_device_ids=true | all-gather | bytes 76800 | tf_op jit(solution)/shard_map/all_gather | solution.py:147
  29.3 15.0 %all-gather.13.cloned.1.call-done = bf16[2560,2,128]{2,0,1:T(8,128)(2,1)} async-done(((bf16[640,2,128]{2,0,1:T(8,128)(2,1)}), bf16[2560,2,128]{2,0,1:T(8,128)(2,1)}) %all-gather.13.cloned.1.call-update) | async-done | bytes 1310736 | tf_op jit(solution)/shard_map/all_gather | solution.py:148
  45.9 16.7 %all-gather.9.cloned.1.call-done = bf16[256,2560]{1,0:T(8,128)(2,1)} async-done(((bf16[256,640]{1,0:T(8,128)(2,1)}), bf16[256,2560]{1,0:T(8,128)(2,1)}) %all-gather.9.cloned.1.call-update) | async-done | bytes 1310736 | tf_op jit(solution)/shard_map/all_gather | solution.py:144
  64.4 1.9 convolution_convert_fusion.6
  66.3 16.2 %all-gather.17.cloned.1.call-done = bf16[256,2560]{1,0:T(8,128)(2,1)} async-done(((bf16[256,640]{1,0:T(8,128)(2,1)}), bf16[256,2560]{1,0:T(8,128)(2,1)}) %all-gather.17.cloned.1.call-update) | async-done | bytes 1310736 | tf_op jit(solution)/shard_map/all_gather | solution.py:175
  82.4 79.0 %all-gather.15.cloned.1.call-done = bf16[768,2560]{1,0:T(8,128)(2,1)} async-done(((bf16[768,640]{1,0:T(8,128)(2,1)}), bf16[768,2560]{1,0:T(8,128)(2,1)}) %all-gather.15.cloned.1.call-update) | async-done | bytes 3932176 | tf_op jit(solution)/shard_map/all_gather | solution.py:170
  161.5 4.5 convolution_convert_fusion.5
  166.0 137.2 %all-gather.11.cloned.1.call-done = bf16[2560,2,768]{2,0,1:T(8,128)(2,1)} async-done(((bf16[640,2,768]{2,0,1:T(8,128)(2,1)}), bf16[2560,2,768]{2,0,1:T(8,128)(2,1)}) %all-gather.11.cloned.1.call-update) | async-done | bytes 7864336 | tf_op jit(solution)/shard_map/all_gather | solution.py:146
  303.1 10.6 %copy.202 = bf16[2560,2,768]{0,2,1:T(8,128)(2,1)} copy(bf16[2560,2,768]{2,0,1:T(8,128)(2,1)} %all-gather.11.cloned.1.call-done) | data formatting | bytes 15728640 | tf_op jit(solution)/shard_map/all_gather | solution.py:146
  313.8 5.5 convolution_convert_fusion.4
  319.6 2.2 reshape.492
  321.8 4.1 fusion.163
  336.6 12.9 %while.149 = (s32[]{:T(128)}, f32[12,64,128]{2,1,0:T(8,128)S(1)}, f32[2,128,12]{2,1,0:T(8,128)}, f32[2,12]{1,0:T(2,128)}, f32[2,12,1,1]{1,3,2,0:T(1,128)}, /*ind...) while((s32[]{:T(128)}, f32[12,64,128]{2,1,0:T(8,128)S(1)}, ...), condition=%wide.region_3.5_spmd.clone, body=%wide.region_1.4_spmd.clone.sunk | while | flops 151785984 | bytes 3003528 | solution.py:100
  349.5 17.9 %all-gather.1 = bf16[48,64,128]{2,1,0:T(8,128)(2,1)S(1)} all-gather(bf16[12,64,128]{2,1,0:T(8,128)(2,1)S(1)} %convert_element_type.154), channel_id=3, replica_groups=mesh['groups'=2,'seq'=4,'head'=4] {'seq'}, dimensions={0}, use_global_device_ids=true | all-gather | bytes 983040 | tf_op jit(solution)/shard_map/all_gather | solution.py:18
  367.6 10.9 %all-reduce.8 = bf16[48]{0:T(256)(128)(2,1)S(1)} all-reduce(bf16[48]{0:T(256)(128)(2,1)S(1)} %dynamic-update-slice), channel_id=2, replica_groups=mesh['groups'=2,'seq'=4,'head'=4] {'seq'}, use_global_device_ids=true, to_apply=%add.8 | all-reduce | flops 48 | bytes 192
  385.6 56.7 %while.148 = (s32[]{:T(128)}, f32[12,64,128]{2,1,0:T(8,128)S(1)}, f32[2,128,12,64]{1,0,3,2:T(2,128)}, f32[2,128,12]{2,1,0:T(8,128)S(1)}, f32[2,12]{1,0:T(2,128)}...) while((s32[]{:T(128)}, f32[12,64,128]{2,1,0:T(8,128)S(1)}, ...), condition=%wide.region_8.10_spmd.clone.clone, body=%wide.region_6.9_spmd.clone.clone.sunk | while | flops 480711168 | bytes 10328741 | solution.py:100
  388.8 2.6 multiply_dynamic-update-slice_fusion.2
  394.8 3.3 fusion.254
  398.1 10.1 %dynamic_update_slice.295 = f32[2,128,12,64]{1,0,3,2:T(2,128)} dynamic-update-slice(f32[2,128,12,64]{1,0,3,2:T(2,128)} %get-tuple-element.3084, f32[1,128,12,64]{1,0,3,2:T(1,128)} %bitcast.628, s32[]{:T(128)} %get-tuple-element.3082, s32[]{:T(128)} %constant.293.clone.1..sunk.1, s32[]{:T(128)} %constant.293.clone.1..sunk.1, s32[]{:T(128)} %constant.293.clone.1..sunk.1) | dynamic-update-slice | bytes 786436 | tf_op jit(solution)/shard_map/jvp()/while/body/jit(dynamic_update_index_in_dim)/dynamic_update_slice | solution.py:100
  417.2 2.5 multiply_dynamic-update-slice_fusion.2
  423.1 3.3 fusion.254
  426.4 10.1 %dynamic_update_slice.295 = f32[2,128,12,64]{1,0,3,2:T(2,128)} dynamic-update-slice(f32[2,128,12,64]{1,0,3,2:T(2,128)} %get-tuple-element.3084, f32[1,128,12,64]{1,0,3,2:T(1,128)} %bitcast.628, s32[]{:T(128)} %get-tuple-element.3082, s32[]{:T(128)} %constant.293.clone.1..sunk.1, s32[]{:T(128)} %constant.293.clone.1..sunk.1, s32[]{:T(128)} %constant.293.clone.1..sunk.1) | dynamic-update-slice | bytes 786436 | tf_op jit(solution)/shard_map/jvp()/while/body/jit(dynamic_update_index_in_dim)/dynamic_update_slice | solution.py:100
  442.2 3.1 copy.217
  445.3 2.4 squeeze.297
  447.7 2.5 multiply_reduce_fusion
  450.2 5.9 psum.49
  456.1 2.1 copy.327
  458.2 2.3 copy.216
  460.5 3.1 fusion.144
  463.6 6.5 psum.50
  470.8 3.1 fusion.147
  480.4 63.8 %while.151 = (s32[]{:T(128)}, f32[12]{0:T(128)}, f32[12,64,128]{2,1,0:T(8,128)S(1)}, f32[2,128,12,64]{1,0,3,2:T(2,128)}, f32[2,128,12]{2,1,0:T(8,128)}, /*index=...) while((s32[]{:T(128)}, f32[12]{0:T(128)}, ...), condition=%wide.region_24.26_spmd.clone, body=%wide.region_14.25_spmd.clone.sunk | while | flops 960458752 | bytes 23068388 | solution.py:100
  482.3 2.0 fusion.271
  487.8 3.7 fusion.275
  493.2 2.0 fusion.274
  495.2 10.2 %dynamic_update_slice.305 = f32[2,128,12,64]{1,0,3,2:T(2,128)} dynamic-update-slice(f32[2,128,12,64]{1,0,3,2:T(2,128)} %get-tuple-element.3174, f32[1,128,12,64]{1,0,3,2:T(1,128)S(1)} %bitcast.622, s32[]{:T(128)S(6)} %sub.278, s32[]{:T(128)} %constant.293.clone.1..sunk.4, s32[]{:T(128)} %constant.293.clone.1..sunk.4, s32[]{:T(128)} %constant.293.clone.1..sunk.4) | dynamic-update-slice | bytes 786436 | tf_op jit(solution)/shard_map/transpose(jvp())/while/body/jit(dynamic_update_index_in_dim)/dynamic_update_slice | solution.py:100
  505.5 1.9 convolution_bitcast_fusion.11
  512.3 1.9 constant_dynamic-slice_fusion.9
  514.2 2.0 fusion.271
  519.7 3.7 fusion.275
  525.1 2.0 fusion.274
  527.1 10.2 %dynamic_update_slice.305 = f32[2,128,12,64]{1,0,3,2:T(2,128)} dynamic-update-slice(f32[2,128,12,64]{1,0,3,2:T(2,128)} %get-tuple-element.3174, f32[1,128,12,64]{1,0,3,2:T(1,128)S(1)} %bitcast.622, s32[]{:T(128)S(6)} %sub.278, s32[]{:T(128)} %constant.293.clone.1..sunk.4, s32[]{:T(128)} %constant.293.clone.1..sunk.4, s32[]{:T(128)} %constant.293.clone.1..sunk.4) | dynamic-update-slice | bytes 786436 | tf_op jit(solution)/shard_map/transpose(jvp())/while/body/jit(dynamic_update_index_in_dim)/dynamic_update_slice | solution.py:100
  537.4 1.9 convolution_bitcast_fusion.11
  544.2 18.1 %all-gather.2 = bf16[48,64,128]{2,1,0:T(8,128)(2,1)S(1)} all-gather(bf16[12,64,128]{2,1,0:T(8,128)(2,1)S(1)} %convert_element_type.159), channel_id=4, replica_groups=mesh['groups'=2,'seq'=4,'head'=4] {'seq'}, dimensions={0}, use_global_device_ids=true | all-gather | bytes 983040 | tf_op jit(solution)/shard_map/all_gather | solution.py:37
  566.7 40.7 %while.147 = (s32[]{:T(128)}, f32[12,64,128]{2,1,0:T(8,128)S(1)}, f32[2,128,12,64]{1,0,3,2:T(2,128)}, f32[2,128,12]{2,1,0:T(8,128)}, f32[2,128,12]{2,1,0:T(8,128...) while((s32[]{:T(128)}, f32[12,64,128]{2,1,0:T(8,128)S(1)}, ...), condition=%wide.region_31.33_spmd, body=%wide.region_27.32_spmd.sunk | while | flops 302782464 | bytes 15091609 | solution.py:100
  578.4 7.8 dynamic_update_slice.284
  598.7 7.8 dynamic_update_slice.284
  620.9 2.1 convolution_bitcast_fusion.6
  625.1 5.8 convolution_bitcast_fusion.5
  632.7 2.5 copy.269
  635.6 3.4 convolution_convert_fusion.2
  640.5 3.2 convolution_convert_fusion.1
  643.7 6.3 copy.273
  651.9 5.3 fusion.132
  659.2 40.2 %concatenate.4 = bf16[2560,1804]{0,1:T(8,128)(2,1)} concatenate(bf16[2560,1536]{0,1:T(8,128)(2,1)} %fusion.132, bf16[2560,12]{0,1:T(8,128)(2,1)S(1)} %fusion.138, bf16[2560,256]{0,1:T(8,128)(2,1)S(1)} %fusion.137), dimensions={1} | concatenate | bytes 18472960 | tf_op jit(solution)/shard_map/concatenate | solution.py:217
  699.4 14.3 %copy.271 = bf16[2560,1804]{1,0:T(8,128)(2,1)} copy(bf16[2560,1804]{0,1:T(8,128)(2,1)} %concatenate.4) | data formatting | bytes 18472960
  714.5 11.6 %all-reduce.9 = (f32[12]{0:T(128)}, f32[12]{0:T(128)}, f32[12]{0:T(128)}, f32[768]{0:T(1024)}) all-reduce(f32[12]{0:T(128)S(1)} %add.249, f32[12]{0:T(128)S(1)} %add_multiply_fusion.2, f32[12]{0:T(128)S(1)} %copy-done.66, f32[768]{0:T(1024)S(1)} %copy-done.67), channel_id=1, replica_groups=mesh['groups'=2,'seq'=4,'head'=4] {'seq'}, use_global_device_ids=true, to_apply=%region_38.40 | all-reduce | flops 804 | bytes 6432 | tf_op jit(solution)/shard_map/psum | solution.py:200
  726.0 1.9 copy.270
  729.8 61.7 %reduce-scatter.19.cloned.1.call-done = bf16[640,768]{1,0:T(8,128)(2,1)} async-done(((bf16[2560,768]{1,0:T(8,128)(2,1)}), bf16[640,768]{1,0:T(8,128)(2,1)}) %reduce-scatter.19.cloned.1.call-update) | async-done | bytes 983056
  794.4 167.3 %reduce-scatter.17.cloned.1.call-done = bf16[640,1804]{1,0:T(8,128)(2,1)} async-done(((bf16[2560,1804]{1,0:T(8,128)(2,1)}), bf16[640,1804]{1,0:T(8,128)(2,1)}) %reduce-scatter.17.cloned.1.call-update) | async-done | bytes 2309136
  961.7 4.0 slice.47
  965.7 5.4 copy.328
  971.1 7.8 copy.247
  (527 shorter events, 156.7 us)
Async XLA Ops:
  7.2 37.1 %all-gather.13.cloned.1.call-start = ((), (), s32[]{:S(2)}) async-start(), calls=%async_computation.6 | async-start | bytes 1638400 | tf_op jit(solution)/shard_map/all_gather | solution.py:148
  9.1 53.5 %all-gather.9.cloned.1.call-start = ((), (), s32[]{:S(2)}) async-start(), calls=%async_computation.4 | async-start | bytes 1638400 | tf_op jit(solution)/shard_map/all_gather | solution.py:144
  9.9 72.5 %all-gather.17.cloned.1.call-start = ((), (), s32[]{:S(2)}) async-start(), calls=%async_computation.8 | async-start | bytes 1638400 | tf_op jit(solution)/shard_map/all_gather | solution.py:175
  10.6 150.9 %all-gather.15.cloned.1.call-start = ((), (), s32[]{:S(2)}) async-start(), calls=%async_computation.7 | async-start | bytes 4915200 | tf_op jit(solution)/shard_map/all_gather | solution.py:170
  11.2 291.9 %all-gather.11.cloned.1.call-start = ((), (), s32[]{:S(2)}) async-start(), calls=%async_computation.5 | async-start | bytes 9830400 | tf_op jit(solution)/shard_map/all_gather | solution.py:146
  13.4 305.8 %copy-start.74 = (f32[12]{0:T(128)}, f32[12]{0:T(128)S(1)}, u32[]{:S(2)}) copy-start(f32[12]{0:T(128)S(1)} %exp.175) | copy-start | bytes 148
  28.6 35.7 %copy-start.37 = (bf16[2560,12]{0,1:T(8,128)(2,1)}, bf16[2560,12]{0,1:T(8,128)(2,1)S(1)}, u32[]{:S(2)}) copy-start(bf16[2560,12]{0,1:T(8,128)(2,1)S(1)} %all_gather.42) | copy-start | bytes 184324
  64.4 254.9 %copy-start.56 = (bf16[256,12]{0,1:T(8,128)(2,1)}, bf16[256,12]{0,1:T(8,128)(2,1)S(1)}, u32[]{:S(2)}) copy-start(bf16[256,12]{0,1:T(8,128)(2,1)S(1)} %convolution_convert_fusion.7) | copy-start | bytes 18436
  166.0 147.8 %copy-start = (bf16[256,2560]{1,0:T(8,128)(2,1)S(1)}, bf16[256,2560]{1,0:T(8,128)(2,1)}, u32[]{:S(2)}) copy-start(bf16[256,2560]{1,0:T(8,128)(2,1)} %all-gather.9.cloned.1.call-done) | copy-start | bytes 3932164
  313.8 5.5 copy-start.72
  319.5 47.9 %copy-start.78 = (f32[12]{0:T(128)}, f32[12]{0:T(128)S(1)}, u32[]{:S(2)}) copy-start(f32[12]{0:T(128)S(1)} %get-tuple-element.2307) | copy-start | bytes 148
  349.5 29.1 %copy-start.4 = (f32[12,64,128]{2,1,0:T(8,128)S(1)}, f32[12,64,128]{2,1,0:T(8,128)}, u32[]{:S(2)}) copy-start(f32[12,64,128]{2,1,0:T(8,128)} %custom-call.1) | copy-start | bytes 1179652
  442.2 5.5 copy-start.14
  456.1 14.7 %copy-start.61 = (f32[256]{0:T(256)}, f32[256]{0:T(256)S(1)}, u32[]{:S(2)}) copy-start(f32[256]{0:T(256)S(1)} %add_rsqrt_fusion) | copy-start | bytes 3076
  485.5 6.3 copy-start.15
  485.5 6.3 copy-start.29
  487.8 5.4 copy-start.68
  493.1 12.3 %copy-start.40 = (f32[2,128,12]{2,1,0:T(8,128)}, f32[2,128,12]{2,1,0:T(8,128)S(1)}, u32[]{:S(2)}) copy-start(f32[2,128,12]{2,1,0:T(8,128)S(1)} %get-tuple-element.3208) | copy-start | bytes 36868 | tf_op jit(solution)/shard_map/transpose(jvp())/while
  493.1 12.3 %copy-start.42 = (f32[2,128,12]{2,1,0:T(8,128)}, f32[2,128,12]{2,1,0:T(8,128)S(1)}, u32[]{:S(2)}) copy-start(f32[2,128,12]{2,1,0:T(8,128)S(1)} %get-tuple-element.3209) | copy-start | bytes 36868 | tf_op jit(solution)/shard_map/transpose(jvp())/while
  493.2 12.3 %copy-start.55 = (f32[2,128,12,1]{1,2,3,0:T(8,128)S(1)}, f32[2,128,12,1]{1,2,3,0:T(8,128)}, u32[]{:S(2)}) copy-start(f32[2,128,12,1]{1,2,3,0:T(8,128)} %get-tuple-element.3214) | copy-start | bytes 36868 | tf_op jit(solution)/shard_map/transpose(jvp())/while
  495.2 12.2 %copy-start.19 = (f32[128,128]{1,0:T(8,128)S(1)}, f32[128,128]{1,0:T(8,128)}, u32[]{:S(2)}) copy-start(f32[128,128]{1,0:T(8,128)} %get-tuple-element.2982) | copy-start | bytes 196612 | tf_op jit(solution)/shard_map/transpose(jvp())/while
  495.2 12.2 %copy-start.36 = (f32[2,128,128]{1,2,0:T(8,128)S(1)}, f32[2,128,128]{1,2,0:T(8,128)}, u32[]{:S(2)}) copy-start(f32[2,128,128]{1,2,0:T(8,128)} %get-tuple-element.3232) | copy-start | bytes 393220 | tf_op jit(solution)/shard_map/transpose(jvp())/while
  495.2 14.8 %copy-start.84 = (f32[2,12,1,1]{1,3,2,0:T(1,128)S(1)}, f32[2,12,1,1]{1,3,2,0:T(1,128)}, u32[]{:S(2)}) copy-start(f32[2,12,1,1]{1,3,2,0:T(1,128)} %get-tuple-element.3216) | copy-start | bytes 292 | tf_op jit(solution)/shard_map/transpose(jvp())/while
  495.2 14.9 %copy-start.9 = (f32[2,128,128]{2,1,0:T(8,128)S(1)}, f32[2,128,128]{2,1,0:T(8,128)}, u32[]{:S(2)}) copy-start(f32[2,128,128]{2,1,0:T(8,128)} %copy-done.8) | copy-start | bytes 393220 | tf_op jit(solution)/shard_map/transpose(jvp())/while
  505.5 6.2 copy-start.60
  505.5 6.2 copy-start.64
  505.5 6.8 copy-start.3
  517.4 6.3 copy-start.15
  517.4 6.3 copy-start.29
  519.7 5.4 copy-start.68
  525.0 12.3 %copy-start.40 = (f32[2,128,12]{2,1,0:T(8,128)}, f32[2,128,12]{2,1,0:T(8,128)S(1)}, u32[]{:S(2)}) copy-start(f32[2,128,12]{2,1,0:T(8,128)S(1)} %get-tuple-element.3208) | copy-start | bytes 36868 | tf_op jit(solution)/shard_map/transpose(jvp())/while
  525.0 12.3 %copy-start.42 = (f32[2,128,12]{2,1,0:T(8,128)}, f32[2,128,12]{2,1,0:T(8,128)S(1)}, u32[]{:S(2)}) copy-start(f32[2,128,12]{2,1,0:T(8,128)S(1)} %get-tuple-element.3209) | copy-start | bytes 36868 | tf_op jit(solution)/shard_map/transpose(jvp())/while
  525.1 12.3 %copy-start.55 = (f32[2,128,12,1]{1,2,3,0:T(8,128)S(1)}, f32[2,128,12,1]{1,2,3,0:T(8,128)}, u32[]{:S(2)}) copy-start(f32[2,128,12,1]{1,2,3,0:T(8,128)} %get-tuple-element.3214) | copy-start | bytes 36868 | tf_op jit(solution)/shard_map/transpose(jvp())/while
  527.1 12.2 %copy-start.19 = (f32[128,128]{1,0:T(8,128)S(1)}, f32[128,128]{1,0:T(8,128)}, u32[]{:S(2)}) copy-start(f32[128,128]{1,0:T(8,128)} %get-tuple-element.2982) | copy-start | bytes 196612 | tf_op jit(solution)/shard_map/transpose(jvp())/while
  527.1 12.2 %copy-start.36 = (f32[2,128,128]{1,2,0:T(8,128)S(1)}, f32[2,128,128]{1,2,0:T(8,128)}, u32[]{:S(2)}) copy-start(f32[2,128,128]{1,2,0:T(8,128)} %get-tuple-element.3232) | copy-start | bytes 393220 | tf_op jit(solution)/shard_map/transpose(jvp())/while
  527.1 14.8 %copy-start.84 = (f32[2,12,1,1]{1,3,2,0:T(1,128)S(1)}, f32[2,12,1,1]{1,3,2,0:T(1,128)}, u32[]{:S(2)}) copy-start(f32[2,12,1,1]{1,3,2,0:T(1,128)} %get-tuple-element.3216) | copy-start | bytes 292 | tf_op jit(solution)/shard_map/transpose(jvp())/while
  527.1 14.8 %copy-start.9 = (f32[2,128,128]{2,1,0:T(8,128)S(1)}, f32[2,128,128]{2,1,0:T(8,128)}, u32[]{:S(2)}) copy-start(f32[2,128,128]{2,1,0:T(8,128)} %copy-done.8) | copy-start | bytes 393220 | tf_op jit(solution)/shard_map/transpose(jvp())/while
  537.4 6.2 copy-start.60
  537.4 6.2 copy-start.64
  537.4 6.8 copy-start.3
  544.2 18.1 %copy-start.83 = (bf16[4,12]{1,0:T(4,128)(2,1)S(1)}, bf16[4,12]{1,0:T(4,128)(2,1)}, u32[]{:S(2)}) copy-start(bf16[4,12]{1,0:T(4,128)(2,1)} %copy-done.82) | copy-start | bytes 292
  571.0 6.4 copy-start.45
  571.0 6.4 copy-start.47
  571.1 7.3 copy-start.22
  573.8 12.3 %copy-start.50 = (f32[2,128,128]{2,1,0:T(8,128)}, f32[2,128,128]{2,1,0:T(8,128)S(1)}, u32[]{:S(2)}) copy-start(f32[2,128,128]{2,1,0:T(8,128)S(1)} %fusion.248) | copy-start | bytes 393220 | tf_op jit(solution)/shard_map/transpose(jvp())/while
  578.3 7.8 copy-start.46
  578.4 7.8 copy-start.48
  591.4 6.4 copy-start.45
  591.4 6.4 copy-start.47
  591.4 7.2 copy-start.22
  594.2 12.3 %copy-start.50 = (f32[2,128,128]{2,1,0:T(8,128)}, f32[2,128,128]{2,1,0:T(8,128)S(1)}, u32[]{:S(2)}) copy-start(f32[2,128,128]{2,1,0:T(8,128)S(1)} %fusion.248) | copy-start | bytes 393220 | tf_op jit(solution)/shard_map/transpose(jvp())/while
  598.7 7.8 copy-start.46
  598.7 7.8 copy-start.48
  607.4 7.8 copy-start.24
  612.4 7.4 copy-start.31
  613.5 6.4 copy-start.33
  623.0 34.2 %all-reduce.12.cloned.1.call-start = ((), (), s32[]{:S(2)}) async-start(), calls=%async_computation.9 | async-start | bytes 262144 | tf_op jit(solution)/shard_map/psum | solution.py:210
  623.6 102.5 %reduce-scatter.15.cloned.1.call-start = ((), (), s32[]{:S(2)}) async-start(), calls=%async_computation.11 | async-start | bytes 1638400
  625.1 5.8 copy-start.25
  625.1 5.8 copy-start.13
  625.1 5.8 copy-start.38
  635.3 92.6 %reduce-scatter.13.cloned.1.call-start = ((), (), s32[]{:S(2)}) async-start(), calls=%async_computation.10 | async-start | bytes 1638400
  640.4 151.0 %reduce-scatter.19.cloned.1.call-start = ((), (), s32[]{:S(2)}) async-start(), calls=%async_computation.13 | async-start | bytes 4915200
  650.1 311.6 %reduce-scatter.17.cloned.1.call-start = ((), (), s32[]{:S(2)}) async-start(), calls=%async_computation.12 | async-start | bytes 12288000
  (67 other events, 156.3 us)
Sparse Core Ops, SparseCore 0:
  10.2 34.1 all-gather.12
  45.9 16.7 all-gather.8
  64.2 18.1 all-gather.16
  83.9 77.5 all-gather.14
  163.5 139.6 all-gather.10
  626.4 29.5 all-reduce.11
  658.7 26.7 reduce-scatter.14
  688.6 26.5 reduce-scatter.12
  717.6 73.8 reduce-scatter.18
  793.8 167.8 reduce-scatter.16
where the time goes:
time: 1010 us; the launch traced here: 991 us
  waiting for transfers between devices  496 us (49%)
  local copies, waits for them, and re-layouts  262 us (26%)
  blocking collectives  84.7 us (8%)
  matrix products  82.3 us (8%)
  other arithmetic  48.4 us (5%)
  between operations  15.9 us (2%)
    unnamed x14, waiting for transfers between devices  231 us
    all_gather x1, waiting for transfers between devices, on_device(): lax.all_gather(w_zx, 'seq', axis=0, tiled=True)  137 us
    all_gather x1, waiting for transfers between devices, on_device(): lax.all_gather(w_out, 'seq', axis=1, tiled=True)  79 us
    dynamic_update_slice x34, local copies, waits for them, and re-layouts, ssd_pass(): final, outs = lax.scan(advance, s_init, parts)  67.6 us
    unnamed x124, local copies, waits for them, and re-layouts  57.8 us
    concatenate x1, local copies, waits for them, and re-layouts, on_device(): jnp.concatenate([jnp.einsum('tr,tc->rc', cols, d_zx, preferred_element_ty...  40.2 us
  transfers between devices with their start and end apart: 10, of which 7 were waited for; matrix products, arithmetic and copies ran while one was open for 11% of the time, Pallas kernels for 0%

commit v1 on v0

--- a/solution.py
+++ b/solution.py
@@ -10,6 +10,7 @@
 
 EPS_NORM = 1e-05
 HIGH = lax.Precision.HIGHEST
+MID = lax.Precision.HIGH
 
 
 def entering(x, axis, combine, identity):
@@ -135,7 +136,7 @@
     return term + jnp.einsum("tc,dc->td", grads[3], flat_bc, preferred_element_type=jnp.float32)
 
 
-def on_device(hidden, w_zx, w_dt, w_bc, dt_bias, a_log, d_skip, norm_gain, w_out, grad_out):
+def weights_moved(hidden, w_zx, w_dt, w_bc, dt_bias, a_log, d_skip, norm_gain, w_out, grad_out):
     tokens = hidden.shape[0]
     wide = HEADS * HDIM
     local_cols = w_zx.shape[1] * w_zx.shape[2]
@@ -244,7 +245,144 @@
     )
 
 
+def mixer_cols(z_t, xr_t, dtr_t, b_in, c_in, dt_bias, a_log, d_skip):
+    nheads, rows = dtr_t.shape
+    blocks = rows // BLOCK
+    width = xr_t.shape[0] // nheads
+    pos = jnp.arange(BLOCK)
+    lower = pos[:, None] >= pos[None, :]
+    x = jax.nn.silu(xr_t).reshape(nheads, width, blocks, BLOCK)
+    dt = jax.nn.softplus(dtr_t + dt_bias[:, None])
+    ld = (-dt * jnp.exp(a_log)[:, None]).reshape(nheads, blocks, BLOCK)
+    dt = dt.reshape(nheads, blocks, BLOCK)
+    cumul = jnp.einsum("hks,ts->hkt", ld, lower.astype(jnp.float32), precision=HIGH)
+    tail = cumul[:, :, -1]
+    b_blk = b_in.reshape(blocks, BLOCK, -1)
+    c_blk = c_in.reshape(blocks, BLOCK, -1)
+    scores = jnp.einsum("ktn,ksn->kts", c_blk, b_blk, precision=MID)
+    gaps = cumul[:, :, :, None] - cumul[:, :, None, :]
+    weights = jnp.exp(jnp.where(lower, gaps, -1e30)) * scores[None] * dt[:, :, None, :]
+    y = jnp.einsum("hkts,hpks->hpkt", weights, x, precision=MID)
+    inflow = jnp.exp(tail[:, :, None] - cumul) * dt
+    fresh = jnp.einsum("hpks,ksn->hkpn", x * inflow[:, None], b_blk, precision=MID)
+    at = jnp.arange(blocks)
+    reach = (at[:, None] > at[None, :]).astype(jnp.float32)
+    ahead = jnp.einsum("hj,kj->hk", tail, reach, precision=HIGH)
+    span = ahead[:, :, None] - (ahead + tail)[:, None, :]
+    carry = jnp.exp(jnp.where(at[:, None] > at[None, :], span, -1e30))
+    state = jnp.einsum("hkj,hjpn->hkpn", carry, fresh, precision=HIGH)
+    y = y + jnp.einsum("ktn,hkpn->hpkt", c_blk, state, precision=MID) * jnp.exp(cumul)[:, None]
+    y = y + d_skip[:, None, None, None] * x
+    return y.reshape(nheads * width, rows) * jax.nn.silu(z_t)
+
+
+def activations_moved(hidden, w_zx, w_dt, w_bc, dt_bias, a_log, d_skip, norm_gain, w_out, grad_out):
+    f32, bf16 = jnp.float32, jnp.bfloat16
+    peers = lax.axis_size("seq")
+    s, h = lax.axis_index("seq"), lax.axis_index("head")
+    tokens = hidden.shape[0]
+    wide = HEADS * HDIM
+    heads = w_dt.shape[1] // peers
+    span = heads * HDIM
+    swap = [(a * peers + b, b * peers + a) for a in range(peers) for b in range(peers)]
+
+    def turned(x):
+        return lax.ppermute(x, ("seq", "head"), swap)
+
+    def mine(x, size):
+        return lax.dynamic_slice_in_dim(x, s * size, size, 0)
+
+    hid = lax.all_gather(turned(hidden), "head", axis=0, tiled=True)
+    gout = lax.all_gather(turned(grad_out), "head", axis=0, tiled=True)
+    w_z, w_x = w_zx[:, 0], w_zx[:, 1]
+    w_b = w_bc.reshape(w_bc.shape[0], -1)
+
+    def scattered(w):
+        part = jnp.einsum("dc,td->ct", w, hid, preferred_element_type=f32).astype(bf16)
+        return lax.psum_scatter(part, "seq", scatter_dimension=0, tiled=True)
+
+    xr_b = scattered(w_x)
+    hid_h = lax.dynamic_slice_in_dim(hid, h * tokens, tokens, 0)
+    bc_part = jnp.dot(hid_h, w_b, preferred_element_type=f32)
+    dt_part = jnp.einsum("dc,td->ct", w_dt, hid, preferred_element_type=f32)
+    bc_h, dtr_all = lax.psum((bc_part, dt_part), "seq")
+    bc_b = lax.all_gather(bc_h.astype(bf16), "head", axis=0, tiled=True)
+    z_b = scattered(w_z)
+    up_part = jnp.einsum("kd,td->kt", w_out, gout, preferred_element_type=f32).astype(bf16)
+    up_b = lax.psum_scatter(up_part, "seq", scatter_dimension=0, tiled=True)
+    dtr_b = mine(dtr_all, heads).astype(bf16)
+    z_b, xr_b, dtr_b, bc_b, up_b = lax.optimization_barrier((z_b, xr_b, dtr_b, bc_b, up_b))
+    states = w_bc.shape[2]
+    bc_f = bc_b.astype(f32)
+    bias, alog, skip = mine(dt_bias, heads), mine(a_log, heads), mine(d_skip, heads)
+    gain = mine(norm_gain, span)[:, None]
+    upstream = up_b.astype(f32)
+    mixed, pull = jax.vjp(
+        mixer_cols, z_b.astype(f32), xr_b.astype(f32), dtr_b.astype(f32),
+        bc_f[:, :states], bc_f[:, states:], bias, alog, skip,
+    )
+    sums = jnp.stack([jnp.sum(mixed * mixed, axis=0), jnp.sum(upstream * gain * mixed, axis=0)])
+    squares, inner = lax.psum(sums, ("seq", "head"))
+    rinv = lax.rsqrt(squares / wide + EPS_NORM)
+    gated = (mixed * rinv[None] * gain).astype(bf16)
+    gated_all = lax.all_gather(gated, "seq", axis=0, tiled=True)
+    grad_mixed = rinv[None] * gain * upstream - mixed * (rinv * rinv * rinv * inner / wide)[None]
+    gain_part = jnp.sum(upstream * mixed * rinv[None], axis=1)
+    d_z, d_xr, d_dtr, d_b, d_c, g_bias, g_alog, g_skip = pull(grad_mixed)
+    dx_all = lax.all_gather(d_xr.astype(bf16), "seq", axis=0, tiled=True)
+    dz_all = lax.all_gather(d_z.astype(bf16), "seq", axis=0, tiled=True)
+    d_bc = lax.psum(jnp.concatenate([d_b, d_c], axis=1).astype(bf16), ("seq", "head")).astype(f32)
+    small = jnp.concatenate([g_bias, g_alog, g_skip, gain_part])
+    small_all, ddt_all = lax.all_gather((small, d_dtr.astype(bf16)), "seq", axis=0)
+    ddt_all = ddt_all.reshape(peers * heads, -1)
+    grad_dtbias, grad_alog, grad_dskip = (
+        small_all[:, i * heads : (i + 1) * heads].reshape(-1) for i in range(3)
+    )
+    grad_gain = small_all[:, 3 * heads :].reshape(-1)
+
+    out_part = jnp.einsum("kt,kd->td", gated_all, w_out, preferred_element_type=f32)
+    layer_out = turned(
+        lax.psum_scatter(out_part.astype(bf16), "head", scatter_dimension=0, tiled=True)
+    )
+    grad_wout = jnp.dot(gated_all, gout, preferred_element_type=f32)
+
+    hid_part = jnp.einsum("ct,dc->td", dx_all, w_x, preferred_element_type=f32)
+    hid_part = hid_part + jnp.einsum("ct,dc->td", dz_all, w_z, preferred_element_type=f32)
+    hid_part = hid_part + jnp.einsum("ct,dc->td", ddt_all, w_dt, preferred_element_type=f32)
+    hid_rows = lax.psum_scatter(hid_part.astype(bf16), "head", scatter_dimension=0, tiled=True)
+    upper, lower_part = split_pair(d_bc)
+    hid_rows = hid_rows.astype(f32)
+    for part in (upper, lower_part):
+        rows = lax.dynamic_slice_in_dim(part, h * tokens, tokens, 0)
+        hid_rows = hid_rows + jnp.einsum("tc,dc->td", rows, w_b, preferred_element_type=f32)
+    grad_hidden = turned(hid_rows.astype(bf16))
+
+    grad_wzx = jnp.stack(
+        [jnp.einsum("td,ct->dc", hid, g, preferred_element_type=f32) for g in (dz_all, dx_all)],
+        axis=1,
+    )
+    grad_wdt = jnp.einsum("td,ct->dc", hid, ddt_all, preferred_element_type=f32)
+    grad_wbc = jnp.einsum("td,tc->dc", hid, upper, preferred_element_type=f32) + jnp.einsum(
+        "td,tc->dc", hid, lower_part, preferred_element_type=f32
+    )
+    return (
+        layer_out,
+        grad_hidden,
+        grad_wzx,
+        grad_wdt,
+        grad_wbc.reshape(w_bc.shape),
+        grad_dtbias,
+        grad_alog,
+        grad_dskip,
+        grad_gain,
+        grad_wout,
+    )
+
+
 def solution(mesh):
+    seq, head = mesh.shape["seq"], mesh.shape["head"]
+    even = seq == head and HEADS % (seq * head) == 0
+    on_device = activations_moved if even else weights_moved
     in_specs = (
         P(("groups", "seq"), "head"),
         P("seq", None, "head"),

time: 1010 us -> 531 us (0.53); the launches traced: 991 us -> 530 us
  local copies, waits for them, and re-layouts: 262 us -> 28.9 us
  waiting for transfers between devices: 496 us -> 298 us
  other arithmetic: 48.4 us -> 11.9 us
  matrix products: 82.3 us -> 64.2 us
  starting transfers between devices: 0.61 us -> 17.4 us
    unnamed x14 -> x11, waiting for transfers between devices: 231 us -> 0.86 us
    all_gather x5, waiting for transfers between devices: 264 us -> 69.2 us  [the longest x1 32.6 us: activations_moved(): dx_all = lax.all_gather(d_xr.astype(bf16), 'seq', axis=0, tiled=True)]
    reduce_scatter x0 -> x5, waiting for transfers between devices: none -> 102 us  [the longest x2 67.1 us: scattered(): return lax.psum_scatter(part, 'seq', scatter_dimension=0, tiled=True)]
    psum x1, waiting for transfers between devices: 0.01 us -> 84.6 us  [activations_moved(): lax.psum(jnp.concatenate([d_b, d_c], axis=1).astype(bf16), ('seq', 'head'))]
    dynamic_update_slice x34 -> x0, local copies, waits for them, and re-layouts: 67.6 us -> none  [ssd_pass(): final, outs = lax.scan(advance, s_init, parts)]
    ppermute x0 -> x4, waiting for transfers between devices: none -> 41.9 us  [turned(): return lax.ppermute(x, ('seq', 'head'), swap)]
    concatenate x1 -> x0, local copies, waits for them, and re-layouts: 40.2 us -> none  [on_device(): jnp.concatenate([jnp.einsum('tr,tc->rc', cols, d_zx, preferred_element_ty...]
    psum x3 -> x2, blocking collectives: 23.9 us -> 63.7 us  [the longest x1 36.2 us: activations_moved(): bc_h, dtr_all = lax.psum((bc_part, dt_part), 'seq')]
  transfers between devices with their start and end apart: 10 -> 15, of which waited for: 7 -> 13; matrix products, arithmetic and copies ran while one was open for 11% -> 16% of each run, Pallas kernels for 0% -> 0%
where the time goes in v1:
time: 531 us; the launch traced here: 530 us
  waiting for transfers between devices  298 us (56%)
  blocking collectives  94.3 us (18%)
  matrix products  64.2 us (12%)
  local copies, waits for them, and re-layouts  28.9 us (5%)
  starting transfers between devices  17.4 us (3%)
  between operations  15.2 us (3%)
  other arithmetic  11.9 us (2%)
    psum x1, waiting for transfers between devices, activations_moved(): lax.psum(jnp.concatenate([d_b, d_c], axis=1).astype(bf16), ('seq', 'head'))  84.6 us
    reduce_scatter x2, waiting for transfers between devices, scattered(): return lax.psum_scatter(part, 'seq', scatter_dimension=0, tiled=True)  67.1 us
    ppermute x4, waiting for transfers between devices, turned(): return lax.ppermute(x, ('seq', 'head'), swap)  41.9 us
    psum x1, blocking collectives, activations_moved(): bc_h, dtr_all = lax.psum((bc_part, dt_part), 'seq')  36.2 us
    all_gather x1, waiting for transfers between devices, activations_moved(): dx_all = lax.all_gather(d_xr.astype(bf16), 'seq', axis=0, tiled=True)  32.6 us
    psum x1, blocking collectives, activations_moved(): squares, inner = lax.psum(sums, ('seq', 'head'))  27.5 us
    reduce_scatter x1, waiting for transfers between devices, activations_moved(): lax.psum_scatter(out_part.astype(bf16), 'head', scatter_dimension=0, tile...  23.3 us
    all_gather x1, waiting for transfers between devices, activations_moved(): gated_all = lax.all_gather(gated, 'seq', axis=0, tiled=True)  20.6 us
  transfers between devices with their start and end apart: 15, of which 13 were waited for; matrix products, arithmetic and copies ran while one was open for 16% of the time, Pallas kernels for 0%

profile of v1, /device:TPU:2, one launch (start us, length us, event | category | flops | bytes accessed | tf_op | source)
XLA Modules:
  0.0 530.1 jit_solution(5554338077364798636)
XLA Ops:
  7.2 4.6 collective-permute-start.1
  11.8 16.6 %collective-permute-done.1 = bf16[256,640]{1,0:T(8,128)(2,1)S(1)} collective-permute-done((bf16[256,640]{1,0:T(8,128)(2,1)}, bf16[256,640]{1,0:T(8,128)(2,1)S(1)}, u32[]{:S(2)}, u32[]{:S(2)}) %collective-permute-start.1) | collective-permute-done | bytes 327712 | tf_op jit(solution)/shard_map/ppermute | solution.py:290
  28.5 0.7 copy-done.30
  29.3 1.9 collective-permute-start
  31.2 14.0 %collective-permute-done = bf16[256,640]{1,0:T(8,128)(2,1)S(1)} collective-permute-done((bf16[256,640]{1,0:T(8,128)(2,1)}, bf16[256,640]{1,0:T(8,128)(2,1)S(1)}, u32[]{:S(2)}, u32[]{:S(2)}) %collective-permute-start) | collective-permute-done | bytes 327712 | tf_op jit(solution)/shard_map/ppermute | solution.py:290
  45.1 0.7 copy-done.29
  45.9 2.6 all-gather.11.cloned.1.call-done
  48.6 4.0 convolution_convert_fusion
  52.7 4.0 fusion.144
  56.6 12.3 %all-gather.9.cloned.1.call-done = bf16[1024,640]{1,0:T(8,128)(2,1)} async-done(((bf16[256,640]{1,0:T(8,128)(2,1)}), bf16[1024,640]{1,0:T(8,128)(2,1)}) %all-gather.9.cloned.1.call-update) | async-done | bytes 1310736 | tf_op jit(solution)/shard_map/all_gather | solution.py:295
  68.9 4.5 convolution_convert_fusion.1
  73.5 1.2 copy-done.1
  74.7 4.1 convolution_convert_fusion.2
  79.7 0.8 dynamic_slice.29
  81.3 36.2 %all-reduce.7 = (bf16[12,1024]{1,0:T(8,128)(2,1)S(1)}, bf16[256,256]{1,0:T(8,128)(2,1)S(1)}) all-reduce(f32[12,1024]{1,0:T(8,128)S(1)} %fusion.148, f32[256,256]{1,0:T(8,128)S(1)} %fusion.82), channel_id=1, replica_groups=mesh['groups'=2,'seq'=4,'head'=4] {'seq'}, use_global_device_ids=true, to_apply=%region_2.0 | all-reduce | flops 77824 | bytes 466944 | tf_op jit(solution)/shard_map/psum | solution.py:308
  117.5 7.0 %all_gather.31 = bf16[1024,256]{1,0:T(8,128)(2,1)S(1)} all-gather(bf16[256,256]{1,0:T(8,128)(2,1)S(1)} %get-tuple-element.69), channel_id=1, replica_groups=mesh['groups'=2,'seq'=4,'head'=4] {'head'}, dimensions={0}, use_global_device_ids=true | all-gather | bytes 655360 | tf_op jit(solution)/shard_map/all_gather | solution.py:309
  124.6 30.7 %reduce-scatter.8.cloned.1.call-done = bf16[192,1024]{1,0:T(8,128)(2,1)} async-done(((bf16[768,1024]{1,0:T(8,128)(2,1)}), bf16[192,1024]{1,0:T(8,128)(2,1)}) %reduce-scatter.8.cloned.1.call-update) | async-done | bytes 393232 | tf_op jit(solution)/shard_map/reduce_scatter | solution.py:302
  155.3 36.4 %reduce-scatter.6.cloned.1.call-done = bf16[192,1024]{1,0:T(8,128)(2,1)} async-done(((bf16[768,1024]{1,0:T(8,128)(2,1)}), bf16[192,1024]{1,0:T(8,128)(2,1)}) %reduce-scatter.6.cloned.1.call-update) | async-done | bytes 393232 | tf_op jit(solution)/shard_map/reduce_scatter | solution.py:302
  192.4 1.2 fusion.79
  194.7 0.9 copy-done.6
  195.6 2.0 fusion.70
  197.6 1.6 convolution_bitcast_fusion.4
  199.3 1.8 fusion.18
  201.6 0.9 copy-done.11
  202.4 1.4 multiply_reduce_fusion.5
  203.8 27.5 %psum.30 = f32[2,1024]{1,0:T(2,128)S(1)} all-reduce(f32[2,1024]{1,0:T(2,128)S(1)} %pad_maximum_fusion.2), channel_id=1, replica_groups=mesh['groups'=2,'seq'=4,'head'=4] {'seq','head'}, use_global_device_ids=true, to_apply=%region_7.8 | all-reduce | flops 2048 | bytes 16384 | tf_op jit(solution)/shard_map/psum | solution.py:325
  231.3 3.7 multiply_reduce_fusion.2
  235.1 1.4 copy.162
  237.1 0.9 copy-done.8
  238.0 1.3 convolution_bitcast_fusion.5
  240.7 1.2 fusion.12
  242.8 1.1 fusion.35
  244.0 0.7 all-gather.13.cloned.1.call-update
  244.8 4.2 fusion.138
  249.0 4.5 fusion.29
  254.3 13.6 %all-gather.2 = bf16[4,3,1024]{2,1,0:T(4,128)(2,1)S(1)} all-gather(bf16[1,3,1024]{2,1,0:T(4,128)(2,1)S(1)} %bitcast.224), channel_id=2, replica_groups=mesh['groups'=2,'seq'=4,'head'=4] {'seq'}, dimensions={0}, use_global_device_ids=true | all-gather | bytes 30720 | tf_op jit(solution)/shard_map/all_gather | solution.py:336
  268.0 2.5 convolution_bitcast_fusion.6
  270.6 1.1 convolution_bitcast_fusion.7
  272.4 0.9 pad_maximum_fusion.1
  273.4 1.1 all-gather.17.cloned.1.call-done
  274.5 5.0 fusion.77
  279.5 32.6 %all-gather.15.cloned.1.call-done = bf16[768,1024]{1,0:T(8,128)(2,1)} async-done(((bf16[192,1024]{1,0:T(8,128)(2,1)}), bf16[768,1024]{1,0:T(8,128)(2,1)}) %all-gather.15.cloned.1.call-update) | async-done | bytes 1572880 | tf_op jit(solution)/shard_map/all_gather | solution.py:332
  312.1 3.6 fusion.78
  315.7 1.7 add_convert_fusion
  319.2 10.0 %all-reduce.1 = f32[804]{0:T(1024)S(1)} all-reduce(f32[804]{0:T(1024)S(1)} %maximum_dynamic-update-slice_fusion), channel_id=3, replica_groups=mesh['groups'=2,'seq'=4,'head'=4] {'seq'}, use_global_device_ids=true, to_apply=%add.1 | all-reduce | flops 804 | bytes 6432
  329.2 20.6 %all-gather.13.cloned.1.call-done = bf16[768,1024]{1,0:T(8,128)(2,1)} async-done(((bf16[192,1024]{1,0:T(8,128)(2,1)}), bf16[768,1024]{1,0:T(8,128)(2,1)}) %all-gather.13.cloned.1.call-update) | async-done | bytes 1572880 | tf_op jit(solution)/shard_map/all_gather | solution.py:328
  349.8 3.9 convolution_convert_fusion.3
  356.3 0.9 convolution_bitcast_fusion.8
  357.3 84.6 %all-reduce.6.cloned.1.call-done = bf16[1024,256]{1,0:T(8,128)(2,1)} async-done(((bf16[1024,256]{1,0:T(8,128)(2,1)}), bf16[1024,256]{1,0:T(8,128)(2,1)}) %all-reduce.6.cloned.1.call-update) | async-done | bytes 524304 | tf_op jit(solution)/shard_map/psum | solution.py:334
  441.9 1.7 fusion.137
  444.2 1.2 copy.141
  445.5 2.9 convolution_bitcast_fusion.1
  448.4 1.4 convolution_bitcast_fusion
  449.8 2.1 pad_maximum_fusion
  451.9 7.9 %copy.140 = f32[640,2,768]{2,1,0:T(2,128)} copy(f32[640,2,768]{0,2,1:T(8,128)} %pad_maximum_fusion) | data formatting | bytes 7864320
  459.8 11.3 %reduce-scatter.14.cloned.1.call-done = bf16[256,640]{1,0:T(8,128)(2,1)} async-done(((bf16[1024,640]{1,0:T(8,128)(2,1)}), bf16[256,640]{1,0:T(8,128)(2,1)}) %reduce-scatter.14.cloned.1.call-update) | async-done | bytes 327696 | tf_op jit(solution)/shard_map/reduce_scatter | solution.py:352
  471.1 1.3 convolution_add_fusion.2
  472.6 5.5 %collective-permute-start.3 = (bf16[256,640]{1,0:T(8,128)(2,1)S(1)}, bf16[256,640]{1,0:T(8,128)(2,1)S(1)}, u32[]{:S(2)}, u32[]{:S(2)}) collective-permute-start(bf16[256,640]{1,0:T(8,128)(2,1)S(1)} %fusion.21), channel_id=1, source_target_pairs={{0,0},{1,4},{2,8},{3,12},{4,1},{5,5},{6,9},{7,13},{8,2},{9,6},{10,... | collective-permute-start | bytes 983048 | tf_op jit(solution)/shard_map/ppermute | solution.py:290
  478.1 23.3 %reduce-scatter.12.cloned.1.call-done = bf16[256,640]{1,0:T(8,128)(2,1)} async-done(((bf16[1024,640]{1,0:T(8,128)(2,1)}), bf16[256,640]{1,0:T(8,128)(2,1)}) %reduce-scatter.12.cloned.1.call-update) | async-done | bytes 327696 | tf_op jit(solution)/shard_map/reduce_scatter | solution.py:345
  501.4 4.9 collective-permute-start.2
  506.4 4.4 fusion.151
  510.8 11.3 %collective-permute-done.2 = bf16[256,640]{1,0:T(8,128)(2,1)S(1)} collective-permute-done((bf16[256,640]{1,0:T(8,128)(2,1)}, bf16[256,640]{1,0:T(8,128)(2,1)S(1)}, u32[]{:S(2)}, u32[]{:S(2)}) %collective-permute-start.2) | collective-permute-done | bytes 327712 | tf_op jit(solution)/shard_map/ppermute | solution.py:290
  522.1 0.7 copy.259
  522.8 0.7 copy.260
  (141 shorter events, 13.7 us)
Async XLA Ops:
  7.2 41.4 %copy-start = (bf16[768,640]{1,0:T(8,128)(2,1)S(1)}, bf16[768,640]{1,0:T(8,128)(2,1)}, u32[]{:S(2)}) copy-start(bf16[768,640]{1,0:T(8,128)(2,1)} %param.18) | copy-start | bytes 2949124
  7.2 41.4 %all-gather.11.cloned.1.call-start = ((), (), s32[]{:S(2)}) async-start(), calls=%async_computation.8 | async-start | bytes 1638400 | tf_op jit(solution)/shard_map/all_gather | solution.py:296
  7.2 21.2 %collective-permute-start.1 = (bf16[256,640]{1,0:T(8,128)(2,1)}, bf16[256,640]{1,0:T(8,128)(2,1)S(1)}, u32[]{:S(2)}, u32[]{:S(2)}) collective-permute-start(bf16[256,640]{1,0:T(8,128)(2,1)} %param.19), channel_id=1, source_target_pairs={{0,0},{1,4},{2,8},{3,12},{4,1},{5,5},{6,9},{7,13},{8,2},{9,6},{10,... | collective-permute-start | bytes 983048 | tf_op jit(solution)/shard_map/ppermute | solution.py:290
  28.5 0.7 copy-start.30
  29.2 39.7 %all-gather.9.cloned.1.call-start = ((), (), s32[]{:S(2)}) async-start(), calls=%async_computation.5 | async-start | bytes 1638400 | tf_op jit(solution)/shard_map/all_gather | solution.py:295
  29.3 15.9 %collective-permute-start = (bf16[256,640]{1,0:T(8,128)(2,1)}, bf16[256,640]{1,0:T(8,128)(2,1)S(1)}, u32[]{:S(2)}, u32[]{:S(2)}) collective-permute-start(bf16[256,640]{1,0:T(8,128)(2,1)} %param.10), channel_id=1, source_target_pairs={{0,0},{1,4},{2,8},{3,12},{4,1},{5,5},{6,9},{7,13},{8,2},{9,6},{10,... | collective-permute-start | bytes 983048 | tf_op jit(solution)/shard_map/ppermute | solution.py:290
  45.1 0.7 copy-start.29
  45.9 78.7 %reduce-scatter.10.cloned.1.call-start = ((), (), s32[]{:S(2)}) async-start(), calls=%async_computation.9 | async-start | bytes 1966080 | tf_op jit(solution)/shard_map/reduce_scatter | solution.py:312
  48.6 4.1 copy-start.2
  52.6 102.7 %reduce-scatter.8.cloned.1.call-start = ((), (), s32[]{:S(2)}) async-start(), calls=%async_computation.7 | async-start | bytes 1966080 | tf_op jit(solution)/shard_map/reduce_scatter | solution.py:302
  73.4 1.3 copy-start.1
  73.4 118.3 %reduce-scatter.6.cloned.1.call-start = ((), (), s32[]{:S(2)}) async-start(), calls=%async_computation.6 | async-start | bytes 1966080 | tf_op jit(solution)/shard_map/reduce_scatter | solution.py:302
  78.9 0.7 copy-start.34
  78.9 0.7 copy-start.35
  78.9 1.6 copy-start.32
  78.9 1.7 copy-start.31
  78.9 2.1 copy-start.20
  78.9 195.6 %all-gather.17.cloned.1.call-start = ((), (), s32[]{:S(2)}) async-start(), calls=%async_computation.13 | async-start | bytes 1966080 | tf_op jit(solution)/shard_map/all_gather | solution.py:333
  191.8 2.6 copy-start.12
  193.8 5.4 %copy-start.3 = (f32[24,8,8,128]{3,2,1,0:T(8,128)}, f32[24,8,8,128]{3,2,1,0:T(8,128)S(1)}, u32[]{:S(2)}) copy-start(f32[24,8,8,128]{3,2,1,0:T(8,128)S(1)} %copy.158) | copy-start | bytes 2359300
  194.3 4.9 copy-start.27
  194.7 0.9 copy-start.6
  199.2 1.8 copy-start.16
  201.1 1.4 copy-start.25
  201.1 1.4 copy-start.26
  201.5 0.9 copy-start.11
  235.0 77.0 %all-gather.15.cloned.1.call-start = ((), (), s32[]{:S(2)}) async-start(), calls=%async_computation.12 | async-start | bytes 1966080 | tf_op jit(solution)/shard_map/all_gather | solution.py:332
  235.1 1.4 copy-start.17
  236.5 3.8 copy-start.18
  236.7 3.3 copy-start.7
  236.7 2.6 copy-start.4
  236.7 2.6 copy-start.13
  237.1 0.9 copy-start.8
  239.3 0.9 copy-start.9
  239.3 1.3 copy-start.28
  241.9 1.0 copy-start.15
  244.0 105.8 %all-gather.13.cloned.1.call-start = ((), (), s32[]{:S(2)}) async-start(), calls=%async_computation.10 | async-start | bytes 1966080 | tf_op jit(solution)/shard_map/all_gather | solution.py:328
  244.7 197.1 %all-reduce.6.cloned.1.call-start = ((), (), s32[]{:S(2)}) async-start(), calls=%async_computation.15 | async-start | bytes 1048576 | tf_op jit(solution)/shard_map/psum | solution.py:334
  244.8 4.2 copy-start.5
  244.8 4.2 copy-start.19
  268.0 2.5 copy-start.10
  270.5 1.1 copy-start.14
  270.6 1.1 copy-start.24
  273.3 197.7 %reduce-scatter.14.cloned.1.call-start = ((), (), s32[]{:S(2)}) async-start(), calls=%async_computation.14 | async-start | bytes 1638400 | tf_op jit(solution)/shard_map/reduce_scatter | solution.py:352
  312.1 3.6 copy-start.23
  315.7 1.8 copy-start.36
  317.5 184.0 %reduce-scatter.12.cloned.1.call-start = ((), (), s32[]{:S(2)}) async-start(), calls=%async_computation.11 | async-start | bytes 1638400 | tf_op jit(solution)/shard_map/reduce_scatter | solution.py:345
  441.9 1.7 copy-start.22
  445.5 2.9 copy-start.33
  451.9 19.1 %copy-start.21 = (bf16[640,2,128]{2,1,0:T(2,128)(2,1)S(1)}, bf16[640,2,128]{2,1,0:T(2,128)(2,1)}, u32[]{:S(2)}) copy-start(bf16[640,2,128]{2,1,0:T(2,128)(2,1)} %param.13) | copy-start | bytes 983044
  472.6 49.5 %collective-permute-start.3 = (bf16[256,640]{1,0:T(8,128)(2,1)S(1)}, bf16[256,640]{1,0:T(8,128)(2,1)S(1)}, u32[]{:S(2)}, u32[]{:S(2)}) collective-permute-start(bf16[256,640]{1,0:T(8,128)(2,1)S(1)} %fusion.21), channel_id=1, source_target_pairs={{0,0},{1,4},{2,8},{3,12},{4,1},{5,5},{6,9},{7,13},{8,2},{9,6},{10,... | collective-permute-start | bytes 983048 | tf_op jit(solution)/shard_map/ppermute | solution.py:290
  501.4 20.7 %collective-permute-start.2 = (bf16[256,640]{1,0:T(8,128)(2,1)}, bf16[256,640]{1,0:T(8,128)(2,1)S(1)}, u32[]{:S(2)}, u32[]{:S(2)}) collective-permute-start(bf16[256,640]{1,0:T(8,128)(2,1)} %reduce-scatter.12.cloned.1.call-done), channel_id=1, source_target_pairs={{0,0},{1,4},{2,8},{3,12},{4,1},{5,5},{6,9},{7,13},{8,2},{9,6},{10,... | collective-permute-start | bytes 983048 | tf_op jit(solution)/shard_map/ppermute | solution.py:290
Sparse Core Ops, SparseCore 0:
  29.3 19.1 all-gather.10
  50.7 18.1 all-gather.8
  71.2 46.8 reduce-scatter.9
  120.8 34.3 reduce-scatter.7
  157.4 34.2 reduce-scatter.5
  235.2 39.2 all-gather.16
  276.1 35.9 all-gather.14
  313.6 36.1 all-gather.12
  353.8 88.0 all-reduce.5
  444.3 26.7 reduce-scatter.13
  474.3 27.0 reduce-scatter.11

commit v2 on v1

--- a/solution.py
+++ b/solution.py
@@ -245,7 +245,7 @@
     )
 
 
-def mixer_cols(z_t, xr_t, dtr_t, b_in, c_in, dt_bias, a_log, d_skip):
+def mixer_cols(z_t, xr_t, dtr_t, b_t, c_t, dt_bias, a_log, d_skip):
     nheads, rows = dtr_t.shape
     blocks = rows // BLOCK
     width = xr_t.shape[0] // nheads
@@ -257,23 +257,49 @@
     dt = dt.reshape(nheads, blocks, BLOCK)
     cumul = jnp.einsum("hks,ts->hkt", ld, lower.astype(jnp.float32), precision=HIGH)
     tail = cumul[:, :, -1]
-    b_blk = b_in.reshape(blocks, BLOCK, -1)
-    c_blk = c_in.reshape(blocks, BLOCK, -1)
-    scores = jnp.einsum("ktn,ksn->kts", c_blk, b_blk, precision=MID)
+    b_blk = b_t.reshape(-1, blocks, BLOCK)
+    c_blk = c_t.reshape(-1, blocks, BLOCK)
+    scores = jnp.einsum("nkt,nks->kts", c_blk, b_blk, precision=MID)
     gaps = cumul[:, :, :, None] - cumul[:, :, None, :]
     weights = jnp.exp(jnp.where(lower, gaps, -1e30)) * scores[None] * dt[:, :, None, :]
     y = jnp.einsum("hkts,hpks->hpkt", weights, x, precision=MID)
     inflow = jnp.exp(tail[:, :, None] - cumul) * dt
-    fresh = jnp.einsum("hpks,ksn->hkpn", x * inflow[:, None], b_blk, precision=MID)
+    fresh = jnp.einsum("hpks,nks->hkpn", x * inflow[:, None], b_blk, precision=MID)
     at = jnp.arange(blocks)
     reach = (at[:, None] > at[None, :]).astype(jnp.float32)
     ahead = jnp.einsum("hj,kj->hk", tail, reach, precision=HIGH)
     span = ahead[:, :, None] - (ahead + tail)[:, None, :]
     carry = jnp.exp(jnp.where(at[:, None] > at[None, :], span, -1e30))
     state = jnp.einsum("hkj,hjpn->hkpn", carry, fresh, precision=HIGH)
-    y = y + jnp.einsum("ktn,hkpn->hpkt", c_blk, state, precision=MID) * jnp.exp(cumul)[:, None]
+    y = y + jnp.einsum("nkt,hkpn->hpkt", c_blk, state, precision=MID) * jnp.exp(cumul)[:, None]
     y = y + d_skip[:, None, None, None] * x
     return y.reshape(nheads * width, rows) * jax.nn.silu(z_t)
+
+
+def shifted(x, k):
+    count = lax.axis_size("head")
+    return lax.ppermute(x, "head", [(i, (i + k) % count) for i in range(count)])
+
+
+def head_gather(x):
+    count, h = lax.axis_size("head"), lax.axis_index("head")
+    rows = x.shape[0]
+    whole = jnp.zeros((count * rows,) + x.shape[1:], x.dtype)
+    for k in range(count):
+        part = shifted(x, k) if k else x
+        whole = lax.dynamic_update_slice_in_dim(whole, part, lax.rem(h + count - k, count) * rows, 0)
+    return whole
+
+
+def head_sum(x, axis):
+    count, h = lax.axis_size("head"), lax.axis_index("head")
+    size = x.shape[axis] // count
+    total = None
+    for k in range(count):
+        part = lax.dynamic_slice_in_dim(x, lax.rem(h + k, count) * size, size, axis)
+        part = (shifted(part, k) if k else part).astype(jnp.float32)
+        total = part if total is None else total + part
+    return total
 
 
 def activations_moved(hidden, w_zx, w_dt, w_bc, dt_bias, a_log, d_skip, norm_gain, w_out, grad_out):
@@ -281,9 +307,13 @@
     peers = lax.axis_size("seq")
     s, h = lax.axis_index("seq"), lax.axis_index("head")
     tokens = hidden.shape[0]
+    rows = tokens * peers
     wide = HEADS * HDIM
     heads = w_dt.shape[1] // peers
     span = heads * HDIM
+    states = w_bc.shape[2]
+    chans = 2 * states // peers
+    lines = chans * tokens // rows
     swap = [(a * peers + b, b * peers + a) for a in range(peers) for b in range(peers)]
 
     def turned(x):
@@ -292,69 +322,82 @@
     def mine(x, size):
         return lax.dynamic_slice_in_dim(x, s * size, size, 0)
 
-    hid = lax.all_gather(turned(hidden), "head", axis=0, tiled=True)
-    gout = lax.all_gather(turned(grad_out), "head", axis=0, tiled=True)
     w_z, w_x = w_zx[:, 0], w_zx[:, 1]
     w_b = w_bc.reshape(w_bc.shape[0], -1)
-
-    def scattered(w):
-        part = jnp.einsum("dc,td->ct", w, hid, preferred_element_type=f32).astype(bf16)
-        return lax.psum_scatter(part, "seq", scatter_dimension=0, tiled=True)
-
-    xr_b = scattered(w_x)
+    hid = head_gather(turned(hidden))
+    grad_out, hid = lax.optimization_barrier((grad_out, hid))
+    gout = head_gather(turned(grad_out))
+
+    def times_hidden(w, cols):
+        return jnp.einsum("dc,td->ct", w, cols, preferred_element_type=f32).astype(bf16)
+
+    x_part = times_hidden(w_x, hid).reshape(peers, span, rows)
     hid_h = lax.dynamic_slice_in_dim(hid, h * tokens, tokens, 0)
-    bc_part = jnp.dot(hid_h, w_b, preferred_element_type=f32)
-    dt_part = jnp.einsum("dc,td->ct", w_dt, hid, preferred_element_type=f32)
-    bc_h, dtr_all = lax.psum((bc_part, dt_part), "seq")
-    bc_b = lax.all_gather(bc_h.astype(bf16), "head", axis=0, tiled=True)
-    z_b = scattered(w_z)
+    bc_part = times_hidden(w_b, hid_h).reshape(peers, lines, rows)
+    dt_part = times_hidden(w_dt, hid).reshape(peers, heads, rows)
+    dt_part = jnp.pad(dt_part, ((0, 0), (0, -heads % 16), (0, 0)))
+    packed = jnp.concatenate([x_part, bc_part, dt_part], axis=1)
+    packed, hid = lax.optimization_barrier((packed, hid))
+    mixed_in = lax.psum_scatter(packed, "seq", scatter_dimension=0, tiled=True)[0]
+    z_b = lax.psum_scatter(times_hidden(w_z, hid), "seq", scatter_dimension=0, tiled=True)
     up_part = jnp.einsum("kd,td->kt", w_out, gout, preferred_element_type=f32).astype(bf16)
     up_b = lax.psum_scatter(up_part, "seq", scatter_dimension=0, tiled=True)
-    dtr_b = mine(dtr_all, heads).astype(bf16)
-    z_b, xr_b, dtr_b, bc_b, up_b = lax.optimization_barrier((z_b, xr_b, dtr_b, bc_b, up_b))
-    states = w_bc.shape[2]
+    xr_b = mixed_in[:span]
+    dtr_b = mixed_in[span + lines : span + lines + heads]
+    bc_b = lax.all_gather(
+        mixed_in[span : span + lines].reshape(chans, tokens), ("seq", "head"), axis=0
+    )
+    bc_b = bc_b.reshape(peers, -1, chans, tokens).transpose(0, 2, 1, 3).reshape(2, states, rows)
     bc_f = bc_b.astype(f32)
     bias, alog, skip = mine(dt_bias, heads), mine(a_log, heads), mine(d_skip, heads)
     gain = mine(norm_gain, span)[:, None]
     upstream = up_b.astype(f32)
     mixed, pull = jax.vjp(
         mixer_cols, z_b.astype(f32), xr_b.astype(f32), dtr_b.astype(f32),
-        bc_f[:, :states], bc_f[:, states:], bias, alog, skip,
+        bc_f[0], bc_f[1], bias, alog, skip,
     )
     sums = jnp.stack([jnp.sum(mixed * mixed, axis=0), jnp.sum(upstream * gain * mixed, axis=0)])
-    squares, inner = lax.psum(sums, ("seq", "head"))
+    squares, inner = lax.psum(lax.psum(sums, "head"), "seq")
     rinv = lax.rsqrt(squares / wide + EPS_NORM)
     gated = (mixed * rinv[None] * gain).astype(bf16)
     gated_all = lax.all_gather(gated, "seq", axis=0, tiled=True)
     grad_mixed = rinv[None] * gain * upstream - mixed * (rinv * rinv * rinv * inner / wide)[None]
     gain_part = jnp.sum(upstream * mixed * rinv[None], axis=1)
     d_z, d_xr, d_dtr, d_b, d_c, g_bias, g_alog, g_skip = pull(grad_mixed)
-    dx_all = lax.all_gather(d_xr.astype(bf16), "seq", axis=0, tiled=True)
     dz_all = lax.all_gather(d_z.astype(bf16), "seq", axis=0, tiled=True)
-    d_bc = lax.psum(jnp.concatenate([d_b, d_c], axis=1).astype(bf16), ("seq", "head")).astype(f32)
+    d_bc_h = head_sum(jnp.concatenate([d_b, d_c], axis=0).astype(bf16), 1)
     small = jnp.concatenate([g_bias, g_alog, g_skip, gain_part])
-    small_all, ddt_all = lax.all_gather((small, d_dtr.astype(bf16)), "seq", axis=0)
-    ddt_all = ddt_all.reshape(peers * heads, -1)
+    fill = -small.shape[0] % rows
+    small = jnp.pad(small, (0, fill)).reshape(-1, rows)
+    misc = jnp.concatenate([d_dtr.astype(bf16), *split_pair(small)], axis=0)
+    misc = jnp.pad(misc, ((0, -misc.shape[0] % 16), (0, 0)))
+    wave = jnp.concatenate(
+        [d_xr.astype(bf16), d_bc_h.astype(bf16).reshape(-1, rows), misc], axis=0
+    )
+    waves = lax.all_gather(wave, "seq", axis=0)
+    dx_all = waves[:, :span].reshape(peers * span, rows)
+    d_bc = jnp.sum(waves[:, span : span + peers * lines].astype(f32), axis=0)
+    d_bc = d_bc.reshape(2 * states, tokens)
+    rest = waves[:, span + peers * lines :]
+    ddt_all = rest[:, :heads].reshape(peers * heads, rows)
+    count = small.shape[0]
+    pair = rest[:, heads : heads + 2 * count].astype(f32)
+    small_all = (pair[:, :count] + pair[:, count:]).reshape(peers, -1)
     grad_dtbias, grad_alog, grad_dskip = (
         small_all[:, i * heads : (i + 1) * heads].reshape(-1) for i in range(3)
     )
-    grad_gain = small_all[:, 3 * heads :].reshape(-1)
+    grad_gain = small_all[:, 3 * heads : 3 * heads + span].reshape(-1)
 
     out_part = jnp.einsum("kt,kd->td", gated_all, w_out, preferred_element_type=f32)
-    layer_out = turned(
-        lax.psum_scatter(out_part.astype(bf16), "head", scatter_dimension=0, tiled=True)
-    )
+    layer_out = turned(head_sum(out_part.astype(bf16), 0).astype(bf16))
     grad_wout = jnp.dot(gated_all, gout, preferred_element_type=f32)
 
-    hid_part = jnp.einsum("ct,dc->td", dx_all, w_x, preferred_element_type=f32)
-    hid_part = hid_part + jnp.einsum("ct,dc->td", dz_all, w_z, preferred_element_type=f32)
+    hid_part = jnp.einsum("ct,dc->td", dz_all, w_z, preferred_element_type=f32)
+    hid_part = hid_part + jnp.einsum("ct,dc->td", dx_all, w_x, preferred_element_type=f32)
     hid_part = hid_part + jnp.einsum("ct,dc->td", ddt_all, w_dt, preferred_element_type=f32)
-    hid_rows = lax.psum_scatter(hid_part.astype(bf16), "head", scatter_dimension=0, tiled=True)
-    upper, lower_part = split_pair(d_bc)
-    hid_rows = hid_rows.astype(f32)
-    for part in (upper, lower_part):
-        rows = lax.dynamic_slice_in_dim(part, h * tokens, tokens, 0)
-        hid_rows = hid_rows + jnp.einsum("tc,dc->td", rows, w_b, preferred_element_type=f32)
+    hid_rows = head_sum(hid_part.astype(bf16), 0)
+    for part in split_pair(d_bc):
+        hid_rows = hid_rows + jnp.einsum("ct,dc->td", part, w_b, preferred_element_type=f32)
     grad_hidden = turned(hid_rows.astype(bf16))
 
     grad_wzx = jnp.stack(
@@ -362,9 +405,8 @@
         axis=1,
     )
     grad_wdt = jnp.einsum("td,ct->dc", hid, ddt_all, preferred_element_type=f32)
-    grad_wbc = jnp.einsum("td,tc->dc", hid, upper, preferred_element_type=f32) + jnp.einsum(
-        "td,tc->dc", hid, lower_part, preferred_element_type=f32
-    )
+    bc_all = lax.all_gather(d_bc.astype(bf16), "head", axis=1, tiled=True)
+    grad_wbc = jnp.einsum("td,ct->dc", hid, bc_all, preferred_element_type=f32)
     return (
         layer_out,
         grad_hidden,

time: 531 us -> 405 us (0.76); the launches traced: 530 us -> 398 us
  waiting for transfers between devices: 298 us -> 163 us
  blocking collectives: 94.3 us -> 58.3 us
  local copies, waits for them, and re-layouts: 28.9 us -> 50.1 us
  other arithmetic: 11.9 us -> 26.6 us
  starting transfers between devices: 17.4 us -> 28.9 us
  matrix products: 64.2 us -> 54.9 us
    reduce_scatter x4 -> x2, waiting for transfers between devices: 102 us -> 0.04 us  [the longest x1 0.02 us: activations_moved(): lax.psum_scatter(times_hidden(w_z, hid), 'seq', scatter_dimension=0, tile...]
    psum x1 -> x0, waiting for transfers between devices: 84.6 us -> none  [activations_moved(): lax.psum(jnp.concatenate([d_b, d_c], axis=1).astype(bf16), ('seq', 'head'))]
    psum x2, blocking collectives: 63.7 us -> 16 us  [activations_moved(): squares, inner = lax.psum(lax.psum(sums, 'head'), 'seq')]
    all_gather x3 -> x1, waiting for transfers between devices: 47.5 us -> 2.56 us  [activations_moved(): waves = lax.all_gather(wave, 'seq', axis=0)]
    ppermute x4, waiting for transfers between devices: 41.9 us -> 85.4 us  [turned(): return lax.ppermute(x, ('seq', 'head'), swap)]
    reduce_scatter x1, waiting for transfers between devices: 0.01 us -> 25.8 us  [activations_moved(): up_b = lax.psum_scatter(up_part, 'seq', scatter_dimension=0, tiled=True)]
    ppermute x0 -> x15, waiting for transfers between devices: none -> 25.6 us  [shifted(): return lax.ppermute(x, 'head', [(i, (i + k) % count) for i in range(count)])]
    all_gather x1, waiting for transfers between devices: 1.14 us -> 24.1 us  [activations_moved(): dz_all = lax.all_gather(d_z.astype(bf16), 'seq', axis=0, tiled=True)]
  transfers between devices with their start and end apart: 15 -> 25, of which waited for: 13 -> 15; matrix products, arithmetic and copies ran while one was open for 16% -> 25% of each run, Pallas kernels for 0% -> 0%
where the time goes in v2:
time: 405 us; the launch traced here: 398 us
  waiting for transfers between devices  163 us (40%)
  blocking collectives  58.3 us (14%)
  matrix products  54.9 us (14%)
  local copies, waits for them, and re-layouts  50.1 us (12%)
  starting transfers between devices  28.9 us (7%)
  other arithmetic  26.6 us (7%)
  between operations  15.6 us (4%)
    ppermute x4, waiting for transfers between devices, turned(): return lax.ppermute(x, ('seq', 'head'), swap)  85.4 us
    all_gather x1, blocking collectives, activations_moved(): lax.all_gather(mixed_in[span:span + lines].reshape(chans, tokens), ('seq'...  25.8 us
    reduce_scatter x1, waiting for transfers between devices, activations_moved(): up_b = lax.psum_scatter(up_part, 'seq', scatter_dimension=0, tiled=True)  25.8 us
    ppermute x15, waiting for transfers between devices, shifted(): return lax.ppermute(x, 'head', [(i, (i + k) % count) for i in range(count)])  25.6 us
    all_gather x1, waiting for transfers between devices, activations_moved(): dz_all = lax.all_gather(d_z.astype(bf16), 'seq', axis=0, tiled=True)  24.1 us
    unnamed x109, local copies, waits for them, and re-layouts  23.9 us
    all_gather x1, blocking collectives, activations_moved(): bc_all = lax.all_gather(d_bc.astype(bf16), 'head', axis=1, tiled=True)  16.4 us
    ppermute x4, starting transfers between devices, turned(): return lax.ppermute(x, ('seq', 'head'), swap)  16.4 us
  transfers between devices with their start and end apart: 25, of which 15 were waited for; matrix products, arithmetic and copies ran while one was open for 25% of the time, Pallas kernels for 0%

profile of v2, /device:TPU:2, one launch (start us, length us, event | category | flops | bytes accessed | tf_op | source)
XLA Modules:
  0.0 397.9 jit_solution(6401642103047068383)
XLA Ops:
  7.2 4.6 %collective-permute-start = (bf16[256,640]{1,0:T(8,128)(2,1)}, bf16[256,640]{1,0:T(8,128)(2,1)S(1)}, u32[]{:S(2)}, u32[]{:S(2)}) collective-permute-start(bf16[256,640]{1,0:T(8,128)(2,1)} %param.10), channel_id=1, source_target_pairs={{0,0},{1,4},{2,8},{3,12},{4,1},{5,5},{6,9},{7,13},{8,2},{9,6},{10,... | collective-permute-start | bytes 983048 | tf_op jit(solution)/shard_map/ppermute | solution.py:320
  11.8 16.7 %collective-permute-done = bf16[256,640]{1,0:T(8,128)(2,1)S(1)} collective-permute-done((bf16[256,640]{1,0:T(8,128)(2,1)}, bf16[256,640]{1,0:T(8,128)(2,1)S(1)}, u32[]{:S(2)}, u32[]{:S(2)}) %collective-permute-start) | collective-permute-done | bytes 327712 | tf_op jit(solution)/shard_map/ppermute | solution.py:320
  28.5 6.6 %fusion.181 = (bf16[640,1,768]{2,1,0:T(2,128)(2,1)}, bf16[640,1,768]{2,1,0:T(2,128)(2,1)}) fusion(bf16[640,2,768]{2,1,0:T(2,128)(2,1)} %param.11), kind=kLoop, calls=%fused_computation.272 | loop fusion | bytes 3932160 | tf_op jit(solution)/shard_map/slice | solution.py:325
  35.1 1.8 collective-permute-start.3
  39.3 2.2 collective-permute-done.3
  42.5 3.0 convolution_convert_fusion.2
  45.5 1.4 fusion.1
  47.0 4.1 %fusion.8 = bf16[768,1024]{0,1:T(8,128)(2,1)} fusion(bf16[1024,640]{1,0:T(8,128)(2,1)S(1)} %constant_dynamic-update-slice_fusion.4, bf16[640,1,768]{2,1,0:T(2,128)(2,1)} %get-tuple-element.78), kind=kOutput, calls=%fused_computation.19 | convolution fusion | flops 1007419392 | bytes 3866624 | tf_op jit(solution)/shard_map/dc,td->ct/dot_general | solution.py:332
  51.1 2.6 copy.212
  54.7 5.8 %collective-permute-start.4 = (bf16[256,640]{1,0:T(8,128)(2,1)S(1)}, bf16[256,640]{1,0:T(8,128)(2,1)S(1)}, u32[]{:S(2)}, u32[]{:S(2)}) collective-permute-start(bf16[256,640]{1,0:T(8,128)(2,1)S(1)} %copy-done.47), channel_id=1, source_target_pairs={{0,0},{1,4},{2,8},{3,12},{4,1},{5,5},{6,9},{7,13},{8,2},{9,6},{10,... | collective-permute-start | bytes 983048 | tf_op jit(solution)/shard_map/ppermute | solution.py:320
  61.2 1.3 dynamic_slice.55
  63.2 32.0 %collective-permute-done.4 = bf16[256,640]{1,0:T(8,128)(2,1)S(1)} collective-permute-done((bf16[256,640]{1,0:T(8,128)(2,1)S(1)}, bf16[256,640]{1,0:T(8,128)(2,1)S(1)}, u32[]{:S(2)}, u32[]{:S(2)}) %collective-permute-start.4) | collective-permute-done | bytes 327712 | tf_op jit(solution)/shard_map/ppermute | solution.py:320
  95.8 1.7 collective-permute-start.7
  97.7 6.3 %collective-permute-done.5 = bf16[256,640]{1,0:T(8,128)(2,1)S(1)} collective-permute-done((bf16[256,640]{1,0:T(8,128)(2,1)S(1)}, bf16[256,640]{1,0:T(8,128)(2,1)S(1)}, u32[]{:S(2)}, u32[]{:S(2)}) %collective-permute-start.5) | collective-permute-done | bytes 327712 | tf_op jit(solution)/shard_map/ppermute | solution.py:281
  104.1 2.3 collective-permute-done.6
  108.5 2.6 fusion.9
  111.1 2.6 copy.214
  114.6 25.8 %all_gather.18 = bf16[16,64,256]{2,1,0:T(8,128)(2,1)S(1)} all-gather(bf16[1,64,256]{2,1,0:T(8,128)(2,1)S(1)} %all_gather_reshape.3), channel_id=1, replica_groups=mesh['groups'=2,'seq'=4,'head'=4] {'seq','head'}, dimensions={0}, use_global_device_ids=true | all-gather | bytes 557056 | tf_op jit(solution)/shard_map/all_gather | solution.py:347
  141.4 1.2 copy.157
  148.5 1.9 fusion.22
  150.8 25.8 %reduce-scatter.12.cloned.1.call-done = bf16[192,1024]{1,0:T(8,128)(2,1)} async-done(((bf16[768,1024]{1,0:T(8,128)(2,1)}), bf16[192,1024]{1,0:T(8,128)(2,1)}) %reduce-scatter.12.cloned.1.call-update) | async-done | bytes 393232 | tf_op jit(solution)/shard_map/reduce_scatter | solution.py:344
  176.6 2.5 multiply_reduce_fusion.4
  179.1 6.1 %psum.14 = f32[2,1024]{1,0:T(2,128)S(1)} all-reduce(f32[2,1024]{1,0:T(2,128)S(1)} %pad_maximum_fusion.2), channel_id=1, replica_groups=mesh['groups'=2,'seq'=4,'head'=4] {'head'}, use_global_device_ids=true, to_apply=%region_5.6 | all-reduce | flops 2048 | bytes 16384 | tf_op jit(solution)/shard_map/psum | solution.py:360
  185.1 9.9 %psum.15 = f32[2,1024]{1,0:T(2,128)S(1)} all-reduce(f32[2,1024]{1,0:T(2,128)S(1)} %psum.14), channel_id=1, replica_groups=mesh['groups'=2,'seq'=4,'head'=4] {'seq'}, use_global_device_ids=true, to_apply=%region_6.7 | all-reduce | flops 2048 | bytes 16384 | tf_op jit(solution)/shard_map/psum | solution.py:360
  195.1 3.9 fusion.46
  199.4 2.1 multiply_reduce_fusion.2
  201.5 1.9 convolution_bitcast_fusion.6
  203.9 1.3 convolution_bitcast_fusion.5
  205.2 1.9 convolution_bitcast_fusion.8
  207.1 2.6 fusion.177
  209.7 1.4 multiply_reduce_fusion.3
  212.2 3.6 fusion.38
  215.9 2.4 fusion.27
  219.8 1.8 copy.188
  221.6 1.8 fusion.26
  224.2 2.7 fusion.16
  228.7 1.5 collective-permute-start.13
  230.2 1.7 collective-permute-start.14
  231.9 1.3 reduce_sum.177
  233.2 1.2 fusion.138
  240.7 2.9 convolution_convert_fusion.3
  245.6 1.7 collective-permute-start.10
  247.9 24.1 %all-gather.7.cloned.1.call-done = bf16[768,1024]{1,0:T(8,128)(2,1)} async-done(((bf16[192,1024]{1,0:T(8,128)(2,1)}), bf16[768,1024]{1,0:T(8,128)(2,1)}) %all-gather.7.cloned.1.call-update) | async-done | bytes 1572880 | tf_op jit(solution)/shard_map/all_gather | solution.py:367
  272.0 5.1 %fusion.85 = f32[1024,640]{1,0:T(8,128)} fusion(bf16[768,1024]{1,0:T(8,128)(2,1)} %all-gather.7.cloned.1.call-done, bf16[640,1,768]{2,1,0:T(2,128)(2,1)} %get-tuple-element.78), kind=kOutput, calls=%fused_computation.132 | convolution fusion | flops 1006632960 | bytes 5177344 | tf_op jit(solution)/shard_map/ct,dc->td/dot_general | solution.py:395
  277.1 2.7 fusion.187
  279.8 1.4 add_convert_fusion.2
  281.2 3.2 collective-permute-start.11
  284.4 2.6 convolution_bitcast_fusion.1
  287.0 35.2 %collective-permute-done.11 = bf16[256,640]{1,0:T(8,128)(2,1)} collective-permute-done((bf16[256,640]{1,0:T(8,128)(2,1)S(1)}, bf16[256,640]{1,0:T(8,128)(2,1)}, u32[]{:S(2)}, u32[]{:S(2)}) %collective-permute-start.11) | collective-permute-done | bytes 327712 | tf_op jit(solution)/shard_map/ppermute | solution.py:320
  322.2 2.6 all-gather.9.cloned.1.call-done
  327.6 2.7 slice.86
  330.7 16.4 %all_gather.23 = bf16[256,1024]{1,0:T(8,128)(2,1)S(1)} all-gather(bf16[256,256]{1,0:T(8,128)(2,1)S(1)} %convert_element_type.253), channel_id=1, replica_groups=mesh['groups'=2,'seq'=4,'head'=4] {'head'}, dimensions={1}, use_global_device_ids=true | all-gather | bytes 655360 | tf_op jit(solution)/shard_map/all_gather | solution.py:408
  349.1 1.5 fusion.84
  351.9 1.7 collective-permute-start.17
  354.6 1.3 convolution_bitcast_fusion
  355.9 4.0 collective-permute-done.15
  359.9 1.9 collective-permute-done.17
  361.7 6.8 %collective-permute-done.16 = bf16[256,640]{1,0:T(8,128)(2,1)S(1)} collective-permute-done((bf16[256,640]{1,0:T(8,128)(2,1)S(1)}, bf16[256,640]{1,0:T(8,128)(2,1)S(1)}, u32[]{:S(2)}, u32[]{:S(2)}) %collective-permute-start.16) | collective-permute-done | bytes 327712 | tf_op jit(solution)/shard_map/ppermute | solution.py:281
  369.0 2.8 collective-permute-start.18
  371.8 2.2 pad_maximum_fusion
  377.6 7.1 %copy.194 = f32[640,2,768]{2,1,0:T(2,128)} copy(f32[640,2,768]{2,0,1:T(8,128)} %pad_maximum_fusion) | data formatting | bytes 7864320
  385.6 1.5 collective-permute-done.18
  387.1 1.7 copy.345
  388.8 1.7 copy.346
  (220 shorter events, 44.1 us)
Async XLA Ops:
  7.2 101.3 %copy-start = (bf16[768,640]{1,0:T(8,128)(2,1)S(1)}, bf16[768,640]{1,0:T(8,128)(2,1)}, u32[]{:S(2)}) copy-start(bf16[768,640]{1,0:T(8,128)(2,1)} %param.18) | copy-start | bytes 2949124
  7.2 106.6 %reduce-scatter.8.cloned.1.call-start = ((), (), s32[]{:S(2)}) async-start(), calls=%async_computation.3 | async-start | bytes 2293760 | tf_op jit(solution)/shard_map/reduce_scatter | solution.py:341
  7.2 21.3 %collective-permute-start = (bf16[256,640]{1,0:T(8,128)(2,1)}, bf16[256,640]{1,0:T(8,128)(2,1)S(1)}, u32[]{:S(2)}, u32[]{:S(2)}) collective-permute-start(bf16[256,640]{1,0:T(8,128)(2,1)} %param.10), channel_id=1, source_target_pairs={{0,0},{1,4},{2,8},{3,12},{4,1},{5,5},{6,9},{7,13},{8,2},{9,6},{10,... | collective-permute-start | bytes 983048 | tf_op jit(solution)/shard_map/ppermute | solution.py:320
  28.5 10.7 %collective-permute-start.2 = (bf16[256,640]{1,0:T(8,128)(2,1)S(1)}, bf16[256,640]{1,0:T(8,128)(2,1)S(1)}, u32[]{:S(2)}, u32[]{:S(2)}) collective-permute-start(bf16[256,640]{1,0:T(8,128)(2,1)S(1)} %collective-permute-done), channel_id=1, source_target_pairs={{0,2},{1,3},{2,0},{3,1},{4,6},{5,7},{6,4},{7,5},{8,10},{9,11},{10,... | collective-permute-start | bytes 983048 | tf_op jit(solution)/shard_map/ppermute | solution.py:281
  28.5 9.7 %collective-permute-start.1 = (bf16[256,640]{1,0:T(8,128)(2,1)S(1)}, bf16[256,640]{1,0:T(8,128)(2,1)}, u32[]{:S(2)}, u32[]{:S(2)}) collective-permute-start(bf16[256,640]{1,0:T(8,128)(2,1)S(1)} %collective-permute-done), channel_id=1, source_target_pairs={{0,1},{1,2},{2,3},{3,0},{4,5},{5,6},{6,7},{7,4},{8,9},{9,10},{10,1... | collective-permute-start | bytes 983048 | tf_op jit(solution)/shard_map/ppermute | solution.py:281
  35.1 6.4 %collective-permute-start.3 = (bf16[256,640]{1,0:T(8,128)(2,1)S(1)}, bf16[256,640]{1,0:T(8,128)(2,1)S(1)}, u32[]{:S(2)}, u32[]{:S(2)}) collective-permute-start(bf16[256,640]{1,0:T(8,128)(2,1)S(1)} %collective-permute-done), channel_id=1, source_target_pairs={{0,3},{1,0},{2,1},{3,2},{4,7},{5,4},{6,5},{7,6},{8,11},{9,8},{10,9... | collective-permute-start | bytes 983048 | tf_op jit(solution)/shard_map/ppermute | solution.py:281
  37.0 4.5 %copy-start.33 = (bf16[640,12]{0,1:T(8,128)(2,1)S(1)}, bf16[640,12]{0,1:T(8,128)(2,1)}, u32[]{:S(2)}) copy-start(bf16[640,12]{0,1:T(8,128)(2,1)} %param.12) | copy-start | bytes 46084
  37.1 5.0 %copy-start.28 = (bf16[640,2,128]{2,1,0:T(2,128)(2,1)S(1)}, bf16[640,2,128]{2,1,0:T(2,128)(2,1)}, u32[]{:S(2)}) copy-start(bf16[640,2,128]{2,1,0:T(2,128)(2,1)} %param.13) | copy-start | bytes 983044
  47.0 103.9 %reduce-scatter.10.cloned.1.call-start = ((), (), s32[]{:S(2)}) async-start(), calls=%async_computation.7 | async-start | bytes 1966080 | tf_op jit(solution)/shard_map/reduce_scatter | solution.py:342
  53.7 6.9 %copy-start.48 = (f32[12]{0:T(128)S(1)}, f32[12]{0:T(128)}, u32[]{:S(2)}) copy-start(f32[12]{0:T(128)} %param.14) | copy-start | bytes 148
  53.7 7.0 %copy-start.49 = (f32[12]{0:T(128)S(1)}, f32[12]{0:T(128)}, u32[]{:S(2)}) copy-start(f32[12]{0:T(128)} %param.16) | copy-start | bytes 148
  53.7 42.1 %copy-start.43 = (f32[12]{0:T(128)S(1)}, f32[12]{0:T(128)}, u32[]{:S(2)}) copy-start(f32[12]{0:T(128)} %param.15) | copy-start | bytes 148
  53.7 122.9 %reduce-scatter.12.cloned.1.call-start = ((), (), s32[]{:S(2)}) async-start(), calls=%async_computation.8 | async-start | bytes 1966080 | tf_op jit(solution)/shard_map/reduce_scatter | solution.py:344
  54.7 40.5 %collective-permute-start.4 = (bf16[256,640]{1,0:T(8,128)(2,1)S(1)}, bf16[256,640]{1,0:T(8,128)(2,1)S(1)}, u32[]{:S(2)}, u32[]{:S(2)}) collective-permute-start(bf16[256,640]{1,0:T(8,128)(2,1)S(1)} %copy-done.47), channel_id=1, source_target_pairs={{0,0},{1,4},{2,8},{3,12},{4,1},{5,5},{6,9},{7,13},{8,2},{9,6},{10,... | collective-permute-start | bytes 983048 | tf_op jit(solution)/shard_map/ppermute | solution.py:320
  60.6 82.3 %copy-start.37 = (f32[3]{0:T(128)}, f32[3]{0:T(128)S(1)}, u32[]{:S(2)}) copy-start(f32[3]{0:T(128)S(1)} %dynamic_slice.52) | copy-start | bytes 40
  95.2 8.8 %collective-permute-start.5 = (bf16[256,640]{1,0:T(8,128)(2,1)S(1)}, bf16[256,640]{1,0:T(8,128)(2,1)S(1)}, u32[]{:S(2)}, u32[]{:S(2)}) collective-permute-start(bf16[256,640]{1,0:T(8,128)(2,1)S(1)} %collective-permute-done.4), channel_id=1, source_target_pairs={{0,1},{1,2},{2,3},{3,0},{4,5},{5,6},{6,7},{7,4},{8,9},{9,10},{10,1... | collective-permute-start | bytes 983048 | tf_op jit(solution)/shard_map/ppermute | solution.py:281
  95.8 10.6 %collective-permute-start.6 = (bf16[256,640]{1,0:T(8,128)(2,1)S(1)}, bf16[256,640]{1,0:T(8,128)(2,1)S(1)}, u32[]{:S(2)}, u32[]{:S(2)}) collective-permute-start(bf16[256,640]{1,0:T(8,128)(2,1)S(1)} %collective-permute-done.4), channel_id=1, source_target_pairs={{0,2},{1,3},{2,0},{3,1},{4,6},{5,7},{6,4},{7,5},{8,10},{9,11},{10,... | collective-permute-start | bytes 983048 | tf_op jit(solution)/shard_map/ppermute | solution.py:281
  95.8 47.3 %copy-start.41 = (f32[3]{0:T(128)}, f32[3]{0:T(128)S(1)}, u32[]{:S(2)}) copy-start(f32[3]{0:T(128)S(1)} %dynamic-slice_exponential_fusion) | copy-start | bytes 40
  95.8 11.5 %collective-permute-start.7 = (bf16[256,640]{1,0:T(8,128)(2,1)S(1)}, bf16[256,640]{1,0:T(8,128)(2,1)S(1)}, u32[]{:S(2)}, u32[]{:S(2)}) collective-permute-start(bf16[256,640]{1,0:T(8,128)(2,1)S(1)} %collective-permute-done.4), channel_id=1, source_target_pairs={{0,3},{1,0},{2,1},{3,2},{4,7},{5,4},{6,5},{7,6},{8,11},{9,8},{10,9... | collective-permute-start | bytes 983048 | tf_op jit(solution)/shard_map/ppermute | solution.py:281
  113.7 127.0 %all-gather.5.cloned.1.call-start = ((), (), s32[]{:S(2)}) async-start(), calls=%async_computation.4 | async-start | bytes 1966080 | tf_op jit(solution)/shard_map/all_gather | solution.py:363
  140.4 2.3 copy-start.9
  142.7 2.7 copy-start.7
  143.0 5.5 %copy-start.11 = (f32[24,8,8,128]{3,2,1,0:T(8,128)}, f32[24,8,8,128]{3,2,1,0:T(8,128)S(1)}, u32[]{:S(2)}) copy-start(f32[24,8,8,128]{3,2,1,0:T(8,128)S(1)} %copy.220) | copy-start | bytes 2359300
  143.0 68.2 %copy-start.31 = (f32[1,3,8,128]{3,1,2,0:T(4,128)}, f32[1,3,8,128]{3,1,2,0:T(4,128)S(1)}, u32[]{:S(2)}) copy-start(f32[1,3,8,128]{3,1,2,0:T(4,128)S(1)} %convert_bitcast_fusion.3) | copy-start | bytes 36868
  143.1 81.1 %copy-start.32 = (f32[3,8,128]{2,1,0:T(8,128)}, f32[3,8,128]{2,1,0:T(8,128)S(1)}, u32[]{:S(2)}) copy-start(f32[3,8,128]{2,1,0:T(8,128)S(1)} %compare_select_fusion.5) | copy-start | bytes 36868
  145.4 3.0 copy-start.20
  145.9 2.5 copy-start.1
  145.9 2.5 copy-start.35
  145.9 2.5 copy-start.44
  148.4 1.9 copy-start.13
  150.3 26.3 %copy-start.39 = (f32[192]{0:T(256)S(1)}, f32[192]{0:T(256)}, u32[]{:S(2)}) copy-start(f32[192]{0:T(256)} %dynamic_slice.55) | copy-start | bytes 2308
  199.2 72.8 %all-gather.7.cloned.1.call-start = ((), (), s32[]{:S(2)}) async-start(), calls=%async_computation.5 | async-start | bytes 1966080 | tf_op jit(solution)/shard_map/all_gather | solution.py:367
  199.4 2.1 copy-start.6
  203.4 1.8 copy-start.4
  203.9 3.2 copy-start.2
  205.2 4.5 %copy-start.8 = (bf16[128,8,128]{2,1,0:T(8,128)(2,1)S(1)}, bf16[128,8,128]{2,1,0:T(8,128)(2,1)}, u32[]{:S(2)}) copy-start(bf16[128,8,128]{2,1,0:T(8,128)(2,1)} %copy-done.7) | copy-start | bytes 786436
  205.2 4.5 %copy-start.12 = (f32[24,8,8,128]{3,2,1,0:T(8,128)S(1)}, f32[24,8,8,128]{3,2,1,0:T(8,128)}, u32[]{:S(2)}) copy-start(f32[24,8,8,128]{3,2,1,0:T(8,128)} %copy-done.11) | copy-start | bytes 2359300
  211.2 4.6 %copy-start.36 = (f32[3,8,128]{2,1,0:T(8,128)}, f32[3,8,128]{2,1,0:T(8,128)S(1)}, u32[]{:S(2)}) copy-start(f32[3,8,128]{2,1,0:T(8,128)S(1)} %get-tuple-element.103) | copy-start | bytes 36868
  212.2 3.6 copy-start.14
  215.9 108.9 %all-gather.9.cloned.1.call-start = ((), (), s32[]{:S(2)}) async-start(), calls=%async_computation.6 | async-start | bytes 2785280 | tf_op jit(solution)/shard_map/all_gather | solution.py:377
  226.9 8.9 %copy-start.10 = (bf16[1,224,1024]{2,1,0:T(8,128)(2,1)S(1)}, bf16[1,224,1024]{2,1,0:T(8,128)(2,1)}, u32[]{:S(2)}) copy-start(bf16[1,224,1024]{2,1,0:T(8,128)(2,1)} %reduce-scatter.8.cloned.1.call-done) | copy-start | bytes 1376260
  228.7 9.8 %collective-permute-start.12 = (bf16[256,256]{1,0:T(8,128)(2,1)}, bf16[256,256]{1,0:T(8,128)(2,1)}, u32[]{:S(2)}, u32[]{:S(2)}) collective-permute-start(bf16[256,256]{1,0:T(8,128)(2,1)} %get-tuple-element.91), channel_id=1, source_target_pairs={{0,1},{1,2},{2,3},{3,0},{4,5},{5,6},{6,7},{7,4},{8,9},{9,10},{10,1... | collective-permute-start | bytes 393224 | tf_op jit(solution)/shard_map/ppermute | solution.py:281
  228.7 9.8 %collective-permute-start.13 = (bf16[256,256]{1,0:T(8,128)(2,1)}, bf16[256,256]{1,0:T(8,128)(2,1)}, u32[]{:S(2)}, u32[]{:S(2)}) collective-permute-start(bf16[256,256]{1,0:T(8,128)(2,1)} %get-tuple-element.92), channel_id=1, source_target_pairs={{0,2},{1,3},{2,0},{3,1},{4,6},{5,7},{6,4},{7,5},{8,10},{9,11},{10,... | collective-permute-start | bytes 393224 | tf_op jit(solution)/shard_map/ppermute | solution.py:281
  230.2 8.3 %collective-permute-start.14 = (bf16[256,256]{1,0:T(8,128)(2,1)}, bf16[256,256]{1,0:T(8,128)(2,1)}, u32[]{:S(2)}, u32[]{:S(2)}) collective-permute-start(bf16[256,256]{1,0:T(8,128)(2,1)} %get-tuple-element.93), channel_id=1, source_target_pairs={{0,3},{1,0},{2,1},{3,2},{4,7},{5,4},{6,5},{7,6},{8,11},{9,8},{10,9... | collective-permute-start | bytes 393224 | tf_op jit(solution)/shard_map/ppermute | solution.py:281
  233.2 4.5 %copy-start.42 = (f32[3]{0:T(128)S(1)}, f32[3]{0:T(128)}, u32[]{:S(2)}) copy-start(f32[3]{0:T(128)} %reduce_sum.177) | copy-start | bytes 40
  233.2 5.4 %copy-start.17 = (bf16[128,1024]{1,0:T(8,128)(2,1)S(1)}, bf16[128,1024]{1,0:T(8,128)(2,1)}, u32[]{:S(2)}) copy-start(bf16[128,1024]{1,0:T(8,128)(2,1)} %copy.188) | copy-start | bytes 786436
  233.2 5.4 %copy-start.19 = (bf16[128,1024]{1,0:T(8,128)(2,1)S(1)}, bf16[128,1024]{1,0:T(8,128)(2,1)}, u32[]{:S(2)}) copy-start(bf16[128,1024]{1,0:T(8,128)(2,1)} %copy.189) | copy-start | bytes 786436
  237.7 2.1 copy-start.25
  245.6 34.2 %collective-permute-start.8 = (bf16[256,640]{1,0:T(8,128)(2,1)}, bf16[256,640]{1,0:T(8,128)(2,1)S(1)}, u32[]{:S(2)}, u32[]{:S(2)}) collective-permute-start(bf16[256,640]{1,0:T(8,128)(2,1)} %get-tuple-element.84), channel_id=1, source_target_pairs={{0,1},{1,2},{2,3},{3,0},{4,5},{5,6},{6,7},{7,4},{8,9},{9,10},{10,1... | collective-permute-start | bytes 983048 | tf_op jit(solution)/shard_map/ppermute | solution.py:281
  245.6 34.2 %collective-permute-start.10 = (bf16[256,640]{1,0:T(8,128)(2,1)}, bf16[256,640]{1,0:T(8,128)(2,1)S(1)}, u32[]{:S(2)}, u32[]{:S(2)}) collective-permute-start(bf16[256,640]{1,0:T(8,128)(2,1)} %get-tuple-element.85), channel_id=1, source_target_pairs={{0,3},{1,0},{2,1},{3,2},{4,7},{5,4},{6,5},{7,6},{8,11},{9,8},{10,9... | collective-permute-start | bytes 983048 | tf_op jit(solution)/shard_map/ppermute | solution.py:281
  247.4 32.4 %collective-permute-start.9 = (bf16[256,640]{1,0:T(8,128)(2,1)S(1)}, bf16[256,640]{1,0:T(8,128)(2,1)}, u32[]{:S(2)}, u32[]{:S(2)}) collective-permute-start(bf16[256,640]{1,0:T(8,128)(2,1)S(1)} %get-tuple-element.86), channel_id=1, source_target_pairs={{0,2},{1,3},{2,0},{3,1},{4,6},{5,7},{6,4},{7,5},{8,10},{9,11},{10,... | collective-permute-start | bytes 983048 | tf_op jit(solution)/shard_map/ppermute | solution.py:281
  272.0 5.1 %copy-start.27 = (bf16[1024,640]{1,0:T(8,128)(2,1)S(1)}, bf16[1024,640]{1,0:T(8,128)(2,1)}, u32[]{:S(2)}) copy-start(bf16[1024,640]{1,0:T(8,128)(2,1)} %copy-done.26) | copy-start | bytes 3932164
  272.0 5.1 %copy-start.45 = (bf16[768,1024]{1,0:T(8,128)(2,1)S(1)}, bf16[768,1024]{1,0:T(8,128)(2,1)}, u32[]{:S(2)}) copy-start(bf16[768,1024]{1,0:T(8,128)(2,1)} %all-gather.5.cloned.1.call-done) | copy-start | bytes 4718596
  279.8 4.6 %copy-start.46 = (bf16[768,1024]{1,0:T(8,128)(2,1)S(1)}, bf16[768,1024]{1,0:T(8,128)(2,1)}, u32[]{:S(2)}) copy-start(bf16[768,1024]{1,0:T(8,128)(2,1)} %all-gather.7.cloned.1.call-done) | copy-start | bytes 4718596
  281.2 40.9 %collective-permute-start.11 = (bf16[256,640]{1,0:T(8,128)(2,1)S(1)}, bf16[256,640]{1,0:T(8,128)(2,1)}, u32[]{:S(2)}, u32[]{:S(2)}) collective-permute-start(bf16[256,640]{1,0:T(8,128)(2,1)S(1)} %add_convert_fusion.2), channel_id=1, source_target_pairs={{0,0},{1,4},{2,8},{3,12},{4,1},{5,5},{6,9},{7,13},{8,2},{9,6},{10,... | collective-permute-start | bytes 983048 | tf_op jit(solution)/shard_map/ppermute | solution.py:320
  330.7 17.1 %copy-start.29 = (bf16[640,2,128]{2,1,0:T(2,128)(2,1)S(1)}, bf16[640,2,128]{2,1,0:T(2,128)(2,1)}, u32[]{:S(2)}) copy-start(bf16[640,2,128]{2,1,0:T(2,128)(2,1)} %param.13) | copy-start | bytes 983044
  347.1 2.0 copy-start.24
  349.1 1.7 copy-start.15
  349.1 1.7 copy-start.34
  351.5 8.4 %collective-permute-start.15 = (bf16[256,640]{1,0:T(8,128)(2,1)S(1)}, bf16[256,640]{1,0:T(8,128)(2,1)S(1)}, u32[]{:S(2)}, u32[]{:S(2)}) collective-permute-start(bf16[256,640]{1,0:T(8,128)(2,1)S(1)} %get-tuple-element.81), channel_id=1, source_target_pairs={{0,1},{1,2},{2,3},{3,0},{4,5},{5,6},{6,7},{7,4},{8,9},{9,10},{10,1... | collective-permute-start | bytes 983048 | tf_op jit(solution)/shard_map/ppermute | solution.py:281
  351.9 9.8 %collective-permute-start.17 = (bf16[256,640]{1,0:T(8,128)(2,1)S(1)}, bf16[256,640]{1,0:T(8,128)(2,1)S(1)}, u32[]{:S(2)}, u32[]{:S(2)}) collective-permute-start(bf16[256,640]{1,0:T(8,128)(2,1)S(1)} %get-tuple-element.82), channel_id=1, source_target_pairs={{0,3},{1,0},{2,1},{3,2},{4,7},{5,4},{6,5},{7,6},{8,11},{9,8},{10,9... | collective-permute-start | bytes 983048 | tf_op jit(solution)/shard_map/ppermute | solution.py:281
  353.6 15.0 %collective-permute-start.16 = (bf16[256,640]{1,0:T(8,128)(2,1)S(1)}, bf16[256,640]{1,0:T(8,128)(2,1)S(1)}, u32[]{:S(2)}, u32[]{:S(2)}) collective-permute-start(bf16[256,640]{1,0:T(8,128)(2,1)S(1)} %get-tuple-element.83), channel_id=1, source_target_pairs={{0,2},{1,3},{2,0},{3,1},{4,6},{5,7},{6,4},{7,5},{8,10},{9,11},{10,... | collective-permute-start | bytes 983048 | tf_op jit(solution)/shard_map/ppermute | solution.py:281
  355.9 15.9 %copy-start.23 = (f32[640,1,768]{2,0,1:T(8,128)S(1)}, f32[640,1,768]{2,0,1:T(8,128)}, u32[]{:S(2)}) copy-start(f32[640,1,768]{2,0,1:T(8,128)} %convolution_bitcast_fusion.1) | copy-start | bytes 5898244
  369.0 18.1 %collective-permute-start.18 = (bf16[256,640]{1,0:T(8,128)(2,1)S(1)}, bf16[256,640]{1,0:T(8,128)(2,1)}, u32[]{:S(2)}, u32[]{:S(2)}) collective-permute-start(bf16[256,640]{1,0:T(8,128)(2,1)S(1)} %add_convert_fusion.1), channel_id=1, source_target_pairs={{0,0},{1,4},{2,8},{3,12},{4,1},{5,5},{6,9},{7,13},{8,2},{9,6},{10,... | collective-permute-start | bytes 983048 | tf_op jit(solution)/shard_map/ppermute | solution.py:320
  (11 other events, 12.4 us)
Sparse Core Ops, SparseCore 0:
  47.1 50.4 reduce-scatter.7
  99.9 39.8 reduce-scatter.9
  142.0 34.5 reduce-scatter.11
  199.3 35.2 all-gather.4
  236.0 35.9 all-gather.6
  274.0 50.7 all-gather.8

commit v3 on v2

--- a/solution.py
+++ b/solution.py
@@ -325,11 +325,11 @@
     w_z, w_x = w_zx[:, 0], w_zx[:, 1]
     w_b = w_bc.reshape(w_bc.shape[0], -1)
     hid = head_gather(turned(hidden))
-    grad_out, hid = lax.optimization_barrier((grad_out, hid))
-    gout = head_gather(turned(grad_out))
+    gout_rows, hid = lax.optimization_barrier((turned(grad_out), hid))
+    gout = head_gather(gout_rows)
 
     def times_hidden(w, cols):
-        return jnp.einsum("dc,td->ct", w, cols, preferred_element_type=f32).astype(bf16)
+        return jnp.einsum("dc,td->ct", w, cols, preferred_element_type=f32)
 
     x_part = times_hidden(w_x, hid).reshape(peers, span, rows)
     hid_h = lax.dynamic_slice_in_dim(hid, h * tokens, tokens, 0)
@@ -339,9 +339,12 @@
     packed = jnp.concatenate([x_part, bc_part, dt_part], axis=1)
     packed, hid = lax.optimization_barrier((packed, hid))
     mixed_in = lax.psum_scatter(packed, "seq", scatter_dimension=0, tiled=True)[0]
-    z_b = lax.psum_scatter(times_hidden(w_z, hid), "seq", scatter_dimension=0, tiled=True)
+    z_part = times_hidden(w_z, hid).reshape(peers, span, rows)
     up_part = jnp.einsum("kd,td->kt", w_out, gout, preferred_element_type=f32).astype(bf16)
-    up_b = lax.psum_scatter(up_part, "seq", scatter_dimension=0, tiled=True)
+    z_up = jnp.concatenate([z_part.astype(bf16), up_part.reshape(peers, span, rows)], axis=1)
+    z_up = lax.psum_scatter(z_up, "seq", scatter_dimension=0, tiled=True)[0]
+    z_b, up_b = z_up[:span], z_up[span:]
+    mixed_in = mixed_in.astype(bf16)
     xr_b = mixed_in[:span]
     dtr_b = mixed_in[span + lines : span + lines + heads]
     bc_b = lax.all_gather(
@@ -360,11 +363,12 @@
     squares, inner = lax.psum(lax.psum(sums, "head"), "seq")
     rinv = lax.rsqrt(squares / wide + EPS_NORM)
     gated = (mixed * rinv[None] * gain).astype(bf16)
-    gated_all = lax.all_gather(gated, "seq", axis=0, tiled=True)
     grad_mixed = rinv[None] * gain * upstream - mixed * (rinv * rinv * rinv * inner / wide)[None]
     gain_part = jnp.sum(upstream * mixed * rinv[None], axis=1)
     d_z, d_xr, d_dtr, d_b, d_c, g_bias, g_alog, g_skip = pull(grad_mixed)
-    dz_all = lax.all_gather(d_z.astype(bf16), "seq", axis=0, tiled=True)
+    first = lax.all_gather(jnp.concatenate([gated, d_z.astype(bf16)], axis=0), "seq", axis=0)
+    gated_all = first[:, :span].reshape(peers * span, rows)
+    dz_all = first[:, span:].reshape(peers * span, rows)
     d_bc_h = head_sum(jnp.concatenate([d_b, d_c], axis=0).astype(bf16), 1)
     small = jnp.concatenate([g_bias, g_alog, g_skip, gain_part])
     fill = -small.shape[0] % rows
@@ -375,6 +379,10 @@
         [d_xr.astype(bf16), d_bc_h.astype(bf16).reshape(-1, rows), misc], axis=0
     )
     waves = lax.all_gather(wave, "seq", axis=0)
+    out_part = jnp.einsum("kt,kd->td", gated_all, w_out, preferred_element_type=f32)
+    out_rows = head_sum(out_part.astype(bf16), 0).astype(bf16)
+    out_rows, waves = lax.optimization_barrier((out_rows, waves))
+    layer_out = turned(out_rows)
     dx_all = waves[:, :span].reshape(peers * span, rows)
     d_bc = jnp.sum(waves[:, span : span + peers * lines].astype(f32), axis=0)
     d_bc = d_bc.reshape(2 * states, tokens)
@@ -388,8 +396,6 @@
     )
     grad_gain = small_all[:, 3 * heads : 3 * heads + span].reshape(-1)
 
-    out_part = jnp.einsum("kt,kd->td", gated_all, w_out, preferred_element_type=f32)
-    layer_out = turned(head_sum(out_part.astype(bf16), 0).astype(bf16))
     grad_wout = jnp.dot(gated_all, gout, preferred_element_type=f32)
 
     hid_part = jnp.einsum("ct,dc->td", dz_all, w_z, preferred_element_type=f32)
@@ -398,15 +404,17 @@
     hid_rows = head_sum(hid_part.astype(bf16), 0)
     for part in split_pair(d_bc):
         hid_rows = hid_rows + jnp.einsum("ct,dc->td", part, w_b, preferred_element_type=f32)
-    grad_hidden = turned(hid_rows.astype(bf16))
-
     grad_wzx = jnp.stack(
         [jnp.einsum("td,ct->dc", hid, g, preferred_element_type=f32) for g in (dz_all, dx_all)],
         axis=1,
     )
+    hid_rows, grad_wzx = lax.optimization_barrier((hid_rows.astype(bf16), grad_wzx))
+    grad_hidden = turned(hid_rows)
     grad_wdt = jnp.einsum("td,ct->dc", hid, ddt_all, preferred_element_type=f32)
-    bc_all = lax.all_gather(d_bc.astype(bf16), "head", axis=1, tiled=True)
-    grad_wbc = jnp.einsum("td,ct->dc", hid, bc_all, preferred_element_type=f32)
+    bc_all = head_gather(d_bc.astype(bf16)).reshape(-1, 2 * states, tokens)
+    grad_wbc = jnp.einsum(
+        "htd,hct->dc", hid.reshape(-1, tokens, hid.shape[1]), bc_all, preferred_element_type=f32
+    )
     return (
         layer_out,
         grad_hidden,

time: 405 us -> 461 us (1.14)
  waiting for transfers between devices: 163 us -> 240 us
  blocking collectives: 58.3 us -> 37.1 us
    reduce_scatter x1, waiting for transfers between devices: 0.02 us -> 68 us  [activations_moved(): lax.psum_scatter(packed, 'seq', scatter_dimension=0, tiled=True)[0]]
    ppermute x4, waiting for transfers between devices: 85.4 us -> 33.8 us  [turned(): return lax.ppermute(x, ('seq', 'head'), swap)]
    reduce_scatter x2 -> x1, waiting for transfers between devices: 25.8 us -> 60.9 us  [activations_moved(): z_up = lax.psum_scatter(z_up, 'seq', scatter_dimension=0, tiled=True)[0]]
    all_gather x1, waiting for transfers between devices: 2.56 us -> 27.3 us  [activations_moved(): waves = lax.all_gather(wave, 'seq', axis=0)]
    all_gather x1 -> x0, blocking collectives: 16.4 us -> none  [activations_moved(): bc_all = lax.all_gather(d_bc.astype(bf16), 'head', axis=1, tiled=True)]
    ppermute x15 -> x18, waiting for transfers between devices: 25.6 us -> 16.8 us  [shifted(): return lax.ppermute(x, 'head', [(i, (i + k) % count) for i in range(count)])]
    unnamed x109 -> x130, local copies, waits for them, and re-layouts: 23.9 us -> 15.3 us
    all_gather x2 -> x1, waiting for transfers between devices: 24.1 us -> 32.3 us  [activations_moved(): lax.all_gather(jnp.concatenate([gated, d_z.astype(bf16)], axis=0), 'seq',...]
  transfers between devices with their start and end apart: 25 -> 26, of which waited for: 15 -> 12; matrix products, arithmetic and copies ran while one was open for 25% -> 22% of each run, Pallas kernels for 0% -> 0%
where the time goes in v3:
time: 461 us; the launch traced here: 453 us
  waiting for transfers between devices  240 us (52%)
  matrix products  52.9 us (11%)
  local copies, waits for them, and re-layouts  49.2 us (11%)
  blocking collectives  37.1 us (8%)
  starting transfers between devices  30 us (7%)
  other arithmetic  29.4 us (6%)
  between operations  15.2 us (3%)
    reduce_scatter x1, waiting for transfers between devices, activations_moved(): lax.psum_scatter(packed, 'seq', scatter_dimension=0, tiled=True)[0]  68 us
    reduce_scatter x1, waiting for transfers between devices, activations_moved(): z_up = lax.psum_scatter(z_up, 'seq', scatter_dimension=0, tiled=True)[0]  60.9 us
    ppermute x4, waiting for transfers between devices, turned(): return lax.ppermute(x, ('seq', 'head'), swap)  33.8 us
    all_gather x1, waiting for transfers between devices, activations_moved(): lax.all_gather(jnp.concatenate([gated, d_z.astype(bf16)], axis=0), 'seq',...  32.3 us
    all_gather x1, waiting for transfers between devices, activations_moved(): waves = lax.all_gather(wave, 'seq', axis=0)  27.3 us
    all_gather x1, blocking collectives, activations_moved(): lax.all_gather(mixed_in[span:span + lines].reshape(chans, tokens), ('seq'...  19.4 us
    psum x2, blocking collectives, activations_moved(): squares, inner = lax.psum(lax.psum(sums, 'head'), 'seq')  17.7 us
    ppermute x18, waiting for transfers between devices, shifted(): return lax.ppermute(x, 'head', [(i, (i + k) % count) for i in range(count)])  16.8 us
  transfers between devices with their start and end apart: 26, of which 12 were waited for; matrix products, arithmetic and copies ran while one was open for 22% of the time, Pallas kernels for 0%

profile of v3, /device:TPU:2, one launch (start us, length us, event | category | flops | bytes accessed | tf_op | source)
XLA Modules:
  0.0 453.5 jit_solution(16261527643371458079)
XLA Ops:
  7.2 4.6 %collective-permute-start.1 = (bf16[256,640]{1,0:T(8,128)(2,1)}, bf16[256,640]{1,0:T(8,128)(2,1)S(1)}, u32[]{:S(2)}, u32[]{:S(2)}) collective-permute-start(bf16[256,640]{1,0:T(8,128)(2,1)} %param.10), channel_id=1, source_target_pairs={{0,0},{1,4},{2,8},{3,12},{4,1},{5,5},{6,9},{7,13},{8,2},{9,6},{10,... | collective-permute-start | bytes 983048 | tf_op jit(solution)/shard_map/ppermute | solution.py:320
  11.8 3.2 collective-permute-start
  15.0 20.8 %collective-permute-done.1 = bf16[256,640]{1,0:T(8,128)(2,1)S(1)} collective-permute-done((bf16[256,640]{1,0:T(8,128)(2,1)}, bf16[256,640]{1,0:T(8,128)(2,1)S(1)}, u32[]{:S(2)}, u32[]{:S(2)}) %collective-permute-start.1) | collective-permute-done | bytes 327712 | tf_op jit(solution)/shard_map/ppermute | solution.py:320
  35.8 6.6 %fusion.182 = (bf16[640,1,768]{2,1,0:T(2,128)(2,1)}, bf16[640,1,768]{2,1,0:T(2,128)(2,1)}) fusion(bf16[640,2,768]{2,1,0:T(2,128)(2,1)} %param.11), kind=kLoop, calls=%fused_computation.276 | loop fusion | bytes 3932160 | tf_op jit(solution)/shard_map/slice | solution.py:325
  42.4 1.8 collective-permute-start.4
  44.4 3.2 collective-permute-done.2
  49.0 1.8 collective-permute-start.7
  50.8 2.1 collective-permute-start.6
  53.9 3.0 fusion.86
  56.9 2.1 select_maximum_fusion
  59.0 3.0 convolution_convert_fusion.1
  62.2 5.5 %collective-permute-done.5 = bf16[256,640]{1,0:T(8,128)(2,1)} collective-permute-done((bf16[256,640]{1,0:T(8,128)(2,1)S(1)}, bf16[256,640]{1,0:T(8,128)(2,1)}, u32[]{:S(2)}, u32[]{:S(2)}) %collective-permute-start.5) | collective-permute-done | bytes 327712 | tf_op jit(solution)/shard_map/ppermute | solution.py:281
  70.8 1.4 convolution_convert_fusion
  72.2 2.0 pad_maximum_fusion.1
  76.2 60.9 %reduce-scatter.5.cloned.1.call-done = bf16[1,384,1024]{2,1,0:T(8,128)(2,1)} async-done(((bf16[4,384,1024]{2,1,0:T(8,128)(2,1)}), bf16[1,384,1024]{2,1,0:T(8,128)(2,1)}) %reduce-scatter.5.cloned.1.call-update) | async-done | bytes 786448 | tf_op jit(solution)/shard_map/reduce_scatter | solution.py:345
  137.1 1.3 convert_bitcast_fusion
  140.5 68.0 %reduce-scatter.3.cloned.1.call-done = f32[1,224,1024]{2,1,0:T(8,128)} async-done(((f32[4,224,1024]{2,1,0:T(8,128)}), f32[1,224,1024]{2,1,0:T(8,128)}) %reduce-scatter.3.cloned.1.call-update) | async-done | bytes 917520 | tf_op jit(solution)/shard_map/reduce_scatter | solution.py:341
  208.5 1.2 convert_element_type.194
  211.5 19.4 %all_gather.15 = bf16[16,64,256]{2,1,0:T(8,128)(2,1)S(1)} all-gather(bf16[1,64,256]{2,1,0:T(8,128)(2,1)S(1)} %all_gather_reshape.3), channel_id=1, replica_groups=mesh['groups'=2,'seq'=4,'head'=4] {'seq','head'}, dimensions={0}, use_global_device_ids=true | all-gather | bytes 557056 | tf_op jit(solution)/shard_map/all_gather | solution.py:350
  232.0 1.2 copy.92
  234.0 1.3 copy.157
  237.0 1.2 fusion.81
  239.5 1.9 multiply_reduce_fusion.5
  242.9 1.3 fusion.44
  244.2 9.2 %psum.14 = f32[2,1024]{1,0:T(2,128)S(1)} all-reduce(f32[2,1024]{1,0:T(2,128)S(1)} %pad_maximum_fusion.4), channel_id=1, replica_groups=mesh['groups'=2,'seq'=4,'head'=4] {'head'}, use_global_device_ids=true, to_apply=%region_4.5 | all-reduce | flops 2048 | bytes 16384 | tf_op jit(solution)/shard_map/psum | solution.py:363
  253.4 8.5 %psum.15 = f32[2,1024]{1,0:T(2,128)S(1)} all-reduce(f32[2,1024]{1,0:T(2,128)S(1)} %psum.14), channel_id=1, replica_groups=mesh['groups'=2,'seq'=4,'head'=4] {'seq'}, use_global_device_ids=true, to_apply=%region_5.6 | all-reduce | flops 2048 | bytes 16384 | tf_op jit(solution)/shard_map/psum | solution.py:363
  262.0 3.7 fusion.48
  267.1 2.1 multiply_bitcast_fusion
  269.7 1.3 convolution_bitcast_fusion.5
  271.0 1.2 multiply_reduce_fusion.3
  272.3 1.2 fusion.12
  273.5 1.4 copy.116
  274.9 2.6 fusion.174
  277.4 3.6 fusion.35
  282.6 2.5 convolution_bitcast_fusion.7
  288.6 1.6 collective-permute-start.13
  290.5 1.3 fusion.175
  297.6 32.3 %all-gather.5.cloned.1.call-done = bf16[1536,1024]{1,0:T(8,128)(2,1)} async-done(((bf16[384,1024]{1,0:T(8,128)(2,1)}), bf16[1536,1024]{1,0:T(8,128)(2,1)}) %all-gather.5.cloned.1.call-update) | async-done | bytes 3145744 | tf_op jit(solution)/shard_map/all_gather | solution.py:369
  329.9 2.2 fusion.181
  332.0 1.5 convolution_convert_fusion.2
  333.7 1.7 collective-permute-start.10
  336.0 2.7 fusion.187
  338.7 3.0 fusion.87
  341.6 2.5 convolution_bitcast_fusion.1
  344.2 6.5 %collective-permute-done.9 = bf16[256,640]{1,0:T(8,128)(2,1)S(1)} collective-permute-done((bf16[256,640]{1,0:T(8,128)(2,1)S(1)}, bf16[256,640]{1,0:T(8,128)(2,1)S(1)}, u32[]{:S(2)}, u32[]{:S(2)}) %collective-permute-start.9) | collective-permute-done | bytes 327712 | tf_op jit(solution)/shard_map/ppermute | solution.py:281
  351.6 27.3 %all-gather.7.cloned.1.call-done = bf16[1088,1024]{1,0:T(8,128)(2,1)} async-done(((bf16[272,1024]{1,0:T(8,128)(2,1)}), bf16[1088,1024]{1,0:T(8,128)(2,1)}) %all-gather.7.cloned.1.call-update) | async-done | bytes 2228240 | tf_op jit(solution)/shard_map/all_gather | solution.py:381
  381.7 2.7 slice.88
  385.2 5.2 %fusion.85 = f32[1024,640]{1,0:T(8,128)} fusion(bf16[768,1024]{1,0:T(8,128)(2,1)} %bitcast.338, bf16[640,1,768]{2,1,0:T(2,128)(2,1)} %get-tuple-element.82), kind=kOutput, calls=%fused_computation.136 | convolution fusion | flops 1006632960 | bytes 5177344 | tf_op jit(solution)/shard_map/ct,dc->td/dot_general | solution.py:402
  390.4 2.5 convolution_bitcast_fusion
  395.0 3.2 add_convert_fusion
  400.3 1.6 collective-permute-start.15
  402.3 1.5 collective-permute-start.16
  403.7 2.2 pad_maximum_fusion
  410.2 1.6 constant_dynamic-update-slice_fusion.2
  411.7 3.1 collective-permute-start.14
  414.9 1.6 constant_dynamic-update-slice_fusion.1
  416.5 1.2 collective-permute-done.16
  417.7 1.6 add_convert_fusion.1
  419.3 4.2 collective-permute-start.18
  424.2 1.7 convolution_bitcast_fusion.6
  426.0 1.3 copy.133
  427.3 5.0 %copy.132 = f32[640,2,768]{2,1,0:T(2,128)} copy(f32[640,2,768]{2,0,1:T(8,128)S(1)} %copy-done.1) | data formatting | bytes 7864320
  432.3 6.9 %collective-permute-done.14 = bf16[256,640]{1,0:T(8,128)(2,1)S(1)} collective-permute-done((bf16[256,640]{1,0:T(8,128)(2,1)}, bf16[256,640]{1,0:T(8,128)(2,1)S(1)}, u32[]{:S(2)}, u32[]{:S(2)}) %collective-permute-start.14) | collective-permute-done | bytes 327712 | tf_op jit(solution)/shard_map/ppermute | solution.py:320
  439.2 6.1 %collective-permute-done.18 = bf16[256,640]{1,0:T(8,128)(2,1)S(1)} collective-permute-done((bf16[256,640]{1,0:T(8,128)(2,1)S(1)}, bf16[256,640]{1,0:T(8,128)(2,1)S(1)}, u32[]{:S(2)}, u32[]{:S(2)}) %collective-permute-start.18) | collective-permute-done | bytes 327712 | tf_op jit(solution)/shard_map/ppermute | solution.py:320
  (247 shorter events, 46.7 us)
Async XLA Ops:
  7.2 63.6 %copy-start = (bf16[768,640]{1,0:T(8,128)(2,1)S(1)}, bf16[768,640]{1,0:T(8,128)(2,1)}, u32[]{:S(2)}) copy-start(bf16[768,640]{1,0:T(8,128)(2,1)} %param.18) | copy-start | bytes 2949124
  7.2 129.9 %reduce-scatter.5.cloned.1.call-start = ((), (), s32[]{:S(2)}) async-start(), calls=%async_computation.3 | async-start | bytes 3932160 | tf_op jit(solution)/shard_map/reduce_scatter | solution.py:345
  7.2 28.6 %collective-permute-start.1 = (bf16[256,640]{1,0:T(8,128)(2,1)}, bf16[256,640]{1,0:T(8,128)(2,1)S(1)}, u32[]{:S(2)}, u32[]{:S(2)}) collective-permute-start(bf16[256,640]{1,0:T(8,128)(2,1)} %param.10), channel_id=1, source_target_pairs={{0,0},{1,4},{2,8},{3,12},{4,1},{5,5},{6,9},{7,13},{8,2},{9,6},{10,... | collective-permute-start | bytes 983048 | tf_op jit(solution)/shard_map/ppermute | solution.py:320
  11.8 37.2 %collective-permute-start = (bf16[256,640]{1,0:T(8,128)(2,1)}, bf16[256,640]{1,0:T(8,128)(2,1)S(1)}, u32[]{:S(2)}, u32[]{:S(2)}) collective-permute-start(bf16[256,640]{1,0:T(8,128)(2,1)} %param.19), channel_id=1, source_target_pairs={{0,0},{1,4},{2,8},{3,12},{4,1},{5,5},{6,9},{7,13},{8,2},{9,6},{10,... | collective-permute-start | bytes 983048 | tf_op jit(solution)/shard_map/ppermute | solution.py:320
  35.8 12.2 %collective-permute-start.3 = (bf16[256,640]{1,0:T(8,128)(2,1)S(1)}, bf16[256,640]{1,0:T(8,128)(2,1)}, u32[]{:S(2)}, u32[]{:S(2)}) collective-permute-start(bf16[256,640]{1,0:T(8,128)(2,1)S(1)} %collective-permute-done.1), channel_id=1, source_target_pairs={{0,2},{1,3},{2,0},{3,1},{4,6},{5,7},{6,4},{7,5},{8,10},{9,11},{10,... | collective-permute-start | bytes 983048 | tf_op jit(solution)/shard_map/ppermute | solution.py:281
  35.8 11.8 %collective-permute-start.2 = (bf16[256,640]{1,0:T(8,128)(2,1)S(1)}, bf16[256,640]{1,0:T(8,128)(2,1)S(1)}, u32[]{:S(2)}, u32[]{:S(2)}) collective-permute-start(bf16[256,640]{1,0:T(8,128)(2,1)S(1)} %collective-permute-done.1), channel_id=1, source_target_pairs={{0,1},{1,2},{2,3},{3,0},{4,5},{5,6},{6,7},{7,4},{8,9},{9,10},{10,1... | collective-permute-start | bytes 983048 | tf_op jit(solution)/shard_map/ppermute | solution.py:281
  42.4 6.5 %collective-permute-start.4 = (bf16[256,640]{1,0:T(8,128)(2,1)S(1)}, bf16[256,640]{1,0:T(8,128)(2,1)S(1)}, u32[]{:S(2)}, u32[]{:S(2)}) collective-permute-start(bf16[256,640]{1,0:T(8,128)(2,1)S(1)} %collective-permute-done.1), channel_id=1, source_target_pairs={{0,3},{1,0},{2,1},{3,2},{4,7},{5,4},{6,5},{7,6},{8,11},{9,8},{10,9... | collective-permute-start | bytes 983048 | tf_op jit(solution)/shard_map/ppermute | solution.py:281
  44.3 8.6 %copy-start.40 = (bf16[640,12]{0,1:T(8,128)(2,1)S(1)}, bf16[640,12]{0,1:T(8,128)(2,1)}, u32[]{:S(2)}) copy-start(bf16[640,12]{0,1:T(8,128)(2,1)} %param.12) | copy-start | bytes 46084
  47.6 5.8 %copy-start.23 = (bf16[640,2,128]{2,1,0:T(2,128)(2,1)S(1)}, bf16[640,2,128]{2,1,0:T(2,128)(2,1)}, u32[]{:S(2)}) copy-start(bf16[640,2,128]{2,1,0:T(2,128)(2,1)} %param.13) | copy-start | bytes 983044
  49.0 20.7 %collective-permute-start.7 = (bf16[256,640]{1,0:T(8,128)(2,1)S(1)}, bf16[256,640]{1,0:T(8,128)(2,1)}, u32[]{:S(2)}, u32[]{:S(2)}) collective-permute-start(bf16[256,640]{1,0:T(8,128)(2,1)S(1)} %collective-permute-done), channel_id=1, source_target_pairs={{0,3},{1,0},{2,1},{3,2},{4,7},{5,4},{6,5},{7,6},{8,11},{9,8},{10,9... | collective-permute-start | bytes 983048 | tf_op jit(solution)/shard_map/ppermute | solution.py:281
  50.8 17.9 %collective-permute-start.6 = (bf16[256,640]{1,0:T(8,128)(2,1)S(1)}, bf16[256,640]{1,0:T(8,128)(2,1)}, u32[]{:S(2)}, u32[]{:S(2)}) collective-permute-start(bf16[256,640]{1,0:T(8,128)(2,1)S(1)} %collective-permute-done), channel_id=1, source_target_pairs={{0,2},{1,3},{2,0},{3,1},{4,6},{5,7},{6,4},{7,5},{8,10},{9,11},{10,... | collective-permute-start | bytes 983048 | tf_op jit(solution)/shard_map/ppermute | solution.py:281
  52.9 14.8 %collective-permute-start.5 = (bf16[256,640]{1,0:T(8,128)(2,1)S(1)}, bf16[256,640]{1,0:T(8,128)(2,1)}, u32[]{:S(2)}, u32[]{:S(2)}) collective-permute-start(bf16[256,640]{1,0:T(8,128)(2,1)S(1)} %collective-permute-done), channel_id=1, source_target_pairs={{0,1},{1,2},{2,3},{3,0},{4,5},{5,6},{6,7},{7,4},{8,9},{9,10},{10,1... | collective-permute-start | bytes 983048 | tf_op jit(solution)/shard_map/ppermute | solution.py:281
  74.3 134.2 %reduce-scatter.3.cloned.1.call-start = ((), (), s32[]{:S(2)}) async-start(), calls=%async_computation.2 | async-start | bytes 4587520 | tf_op jit(solution)/shard_map/reduce_scatter | solution.py:341
  75.0 254.8 %all-gather.5.cloned.1.call-start = ((), (), s32[]{:S(2)}) async-start(), calls=%async_computation.4 | async-start | bytes 3932160 | tf_op jit(solution)/shard_map/all_gather | solution.py:369
  75.2 135.7 %copy-start.54 = (f32[3]{0:T(128)}, f32[3]{0:T(128)S(1)}, u32[]{:S(2)}) copy-start(f32[3]{0:T(128)S(1)} %dynamic_slice.52) | copy-start | bytes 40
  76.2 134.7 %copy-start.56 = (f32[3]{0:T(128)}, f32[3]{0:T(128)S(1)}, u32[]{:S(2)}) copy-start(f32[3]{0:T(128)S(1)} %dynamic-slice_exponential_fusion) | copy-start | bytes 40
  209.7 22.2 %copy-start.16 = (bf16[1,224,1024]{2,1,0:T(8,128)(2,1)}, bf16[1,224,1024]{2,1,0:T(8,128)(2,1)S(1)}, u32[]{:S(2)}) copy-start(bf16[1,224,1024]{2,1,0:T(8,128)(2,1)S(1)} %convert_element_type.194) | copy-start | bytes 1376260
  236.5 3.0 copy-start.37
  237.0 2.5 copy-start.5
  237.0 2.5 copy-start.21
  241.4 2.8 copy-start.22
  241.9 2.3 copy-start.11
  266.6 112.3 %all-gather.7.cloned.1.call-start = ((), (), s32[]{:S(2)}) async-start(), calls=%async_computation.5 | async-start | bytes 2785280 | tf_op jit(solution)/shard_map/all_gather | solution.py:381
  281.0 4.0 copy-start.3
  282.6 2.5 copy-start.9
  286.7 3.5 copy-start.42
  286.8 3.5 copy-start.43
  286.8 3.5 copy-start.44
  286.8 3.4 copy-start.46
  286.8 3.4 copy-start.47
  286.8 3.6 copy-start.17
  286.8 3.6 copy-start.41
  286.8 3.6 copy-start.55
  286.8 3.6 copy-start.57
  287.3 6.8 %copy-start.20 = (f32[3,64,8,128]{3,2,1,0:T(8,128)S(1)}, f32[3,64,8,128]{3,2,1,0:T(8,128)}, u32[]{:S(2)}) copy-start(f32[3,64,8,128]{3,2,1,0:T(8,128)} %copy.116) | copy-start | bytes 2359300
  288.2 7.1 %collective-permute-start.11 = (bf16[256,256]{0,1:T(8,128)(2,1)}, bf16[256,256]{0,1:T(8,128)(2,1)}, u32[]{:S(2)}, u32[]{:S(2)}) collective-permute-start(bf16[256,256]{0,1:T(8,128)(2,1)} %get-tuple-element.94), channel_id=1, source_target_pairs={{0,1},{1,2},{2,3},{3,0},{4,5},{5,6},{6,7},{7,4},{8,9},{9,10},{10,1... | collective-permute-start | bytes 393224 | tf_op jit(solution)/shard_map/ppermute | solution.py:281
  288.2 7.1 %collective-permute-start.12 = (bf16[256,256]{0,1:T(8,128)(2,1)}, bf16[256,256]{0,1:T(8,128)(2,1)}, u32[]{:S(2)}, u32[]{:S(2)}) collective-permute-start(bf16[256,256]{0,1:T(8,128)(2,1)} %get-tuple-element.95), channel_id=1, source_target_pairs={{0,2},{1,3},{2,0},{3,1},{4,6},{5,7},{6,4},{7,5},{8,10},{9,11},{10,... | collective-permute-start | bytes 393224 | tf_op jit(solution)/shard_map/ppermute | solution.py:281
  288.6 6.7 %collective-permute-start.13 = (bf16[256,256]{0,1:T(8,128)(2,1)}, bf16[256,256]{0,1:T(8,128)(2,1)}, u32[]{:S(2)}, u32[]{:S(2)}) collective-permute-start(bf16[256,256]{0,1:T(8,128)(2,1)} %get-tuple-element.96), channel_id=1, source_target_pairs={{0,3},{1,0},{2,1},{3,2},{4,7},{5,4},{6,5},{7,6},{8,11},{9,8},{10,9... | collective-permute-start | bytes 393224 | tf_op jit(solution)/shard_map/ppermute | solution.py:281
  292.5 2.7 copy-start.48
  292.5 2.7 copy-start.52
  292.5 2.7 copy-start.53
  292.5 2.8 copy-start.45
  292.5 2.9 copy-start.26
  292.5 2.9 copy-start.28
  333.5 2.5 copy-start.36
  333.6 10.5 %collective-permute-start.8 = (bf16[256,640]{1,0:T(8,128)(2,1)S(1)}, bf16[256,640]{1,0:T(8,128)(2,1)S(1)}, u32[]{:S(2)}, u32[]{:S(2)}) collective-permute-start(bf16[256,640]{1,0:T(8,128)(2,1)S(1)} %get-tuple-element.88), channel_id=1, source_target_pairs={{0,1},{1,2},{2,3},{3,0},{4,5},{5,6},{6,7},{7,4},{8,9},{9,10},{10,1... | collective-permute-start | bytes 983048 | tf_op jit(solution)/shard_map/ppermute | solution.py:281
  333.7 10.5 %collective-permute-start.10 = (bf16[256,640]{1,0:T(8,128)(2,1)S(1)}, bf16[256,640]{1,0:T(8,128)(2,1)S(1)}, u32[]{:S(2)}, u32[]{:S(2)}) collective-permute-start(bf16[256,640]{1,0:T(8,128)(2,1)S(1)} %get-tuple-element.89), channel_id=1, source_target_pairs={{0,3},{1,0},{2,1},{3,2},{4,7},{5,4},{6,5},{7,6},{8,11},{9,8},{10,9... | collective-permute-start | bytes 983048 | tf_op jit(solution)/shard_map/ppermute | solution.py:281
  335.4 3.2 copy-start.30
  335.4 15.3 %collective-permute-start.9 = (bf16[256,640]{1,0:T(8,128)(2,1)S(1)}, bf16[256,640]{1,0:T(8,128)(2,1)S(1)}, u32[]{:S(2)}, u32[]{:S(2)}) collective-permute-start(bf16[256,640]{1,0:T(8,128)(2,1)S(1)} %get-tuple-element.90), channel_id=1, source_target_pairs={{0,2},{1,3},{2,0},{3,1},{4,6},{5,7},{6,4},{7,5},{8,10},{9,11},{10,... | collective-permute-start | bytes 983048 | tf_op jit(solution)/shard_map/ppermute | solution.py:281
  384.6 27.2 %collective-permute-start.20 = (bf16[256,256]{1,0:T(8,128)(2,1)S(1)}, bf16[256,256]{1,0:T(8,128)(2,1)}, u32[]{:S(2)}, u32[]{:S(2)}) collective-permute-start(bf16[256,256]{1,0:T(8,128)(2,1)S(1)} %convert_element_type.239), channel_id=1, source_target_pairs={{0,2},{1,3},{2,0},{3,1},{4,6},{5,7},{6,4},{7,5},{8,10},{9,11},{10,... | collective-permute-start | bytes 393224 | tf_op jit(solution)/shard_map/ppermute | solution.py:281
  385.2 24.7 %collective-permute-start.19 = (bf16[256,256]{1,0:T(8,128)(2,1)S(1)}, bf16[256,256]{1,0:T(8,128)(2,1)}, u32[]{:S(2)}, u32[]{:S(2)}) collective-permute-start(bf16[256,256]{1,0:T(8,128)(2,1)S(1)} %convert_element_type.239), channel_id=1, source_target_pairs={{0,1},{1,2},{2,3},{3,0},{4,5},{5,6},{6,7},{7,4},{8,9},{9,10},{10,1... | collective-permute-start | bytes 393224 | tf_op jit(solution)/shard_map/ppermute | solution.py:281
  385.2 5.2 %copy-start.33 = (bf16[4,192,1024]{2,1,0:T(8,128)(2,1)S(1)}, bf16[4,192,1024]{2,1,0:T(8,128)(2,1)}, u32[]{:S(2)}) copy-start(bf16[4,192,1024]{2,1,0:T(8,128)(2,1)} %slice.88) | copy-start | bytes 4718596
  395.0 8.8 %copy-start.32 = (f32[640,1,768]{2,0,1:T(8,128)S(1)}, f32[640,1,768]{2,0,1:T(8,128)}, u32[]{:S(2)}) copy-start(f32[640,1,768]{2,0,1:T(8,128)} %convolution_bitcast_fusion) | copy-start | bytes 5898244
  399.3 4.4 copy-start.31
  400.3 16.1 %collective-permute-start.15 = (bf16[256,640]{1,0:T(8,128)(2,1)}, bf16[256,640]{1,0:T(8,128)(2,1)}, u32[]{:S(2)}, u32[]{:S(2)}) collective-permute-start(bf16[256,640]{1,0:T(8,128)(2,1)} %get-tuple-element.85), channel_id=1, source_target_pairs={{0,1},{1,2},{2,3},{3,0},{4,5},{5,6},{6,7},{7,4},{8,9},{9,10},{10,1... | collective-permute-start | bytes 983048 | tf_op jit(solution)/shard_map/ppermute | solution.py:281
  401.9 14.6 %collective-permute-start.17 = (bf16[256,640]{1,0:T(8,128)(2,1)}, bf16[256,640]{1,0:T(8,128)(2,1)}, u32[]{:S(2)}, u32[]{:S(2)}) collective-permute-start(bf16[256,640]{1,0:T(8,128)(2,1)} %get-tuple-element.86), channel_id=1, source_target_pairs={{0,3},{1,0},{2,1},{3,2},{4,7},{5,4},{6,5},{7,6},{8,11},{9,8},{10,9... | collective-permute-start | bytes 983048 | tf_op jit(solution)/shard_map/ppermute | solution.py:281
  402.3 5.2 %copy-start.51 = (f32[4,3]{1,0:T(4,128)S(1)}, f32[4,3]{1,0:T(4,128)}, u32[]{:S(2)}) copy-start(f32[4,3]{1,0:T(4,128)} %get-tuple-element.103) | copy-start | bytes 148
  402.3 6.5 %copy-start.50 = (f32[4,3]{1,0:T(4,128)S(1)}, f32[4,3]{1,0:T(4,128)}, u32[]{:S(2)}) copy-start(f32[4,3]{1,0:T(4,128)} %get-tuple-element.104) | copy-start | bytes 148
  402.3 7.1 %copy-start.49 = (f32[4,3]{1,0:T(4,128)S(1)}, f32[4,3]{1,0:T(4,128)}, u32[]{:S(2)}) copy-start(f32[4,3]{1,0:T(4,128)} %get-tuple-element.105) | copy-start | bytes 148
  402.3 15.4 %collective-permute-start.16 = (bf16[256,640]{1,0:T(8,128)(2,1)}, bf16[256,640]{1,0:T(8,128)(2,1)}, u32[]{:S(2)}, u32[]{:S(2)}) collective-permute-start(bf16[256,640]{1,0:T(8,128)(2,1)} %get-tuple-element.87), channel_id=1, source_target_pairs={{0,2},{1,3},{2,0},{3,1},{4,6},{5,7},{6,4},{7,5},{8,10},{9,11},{10,... | collective-permute-start | bytes 983048 | tf_op jit(solution)/shard_map/ppermute | solution.py:281
  409.9 13.6 %collective-permute-start.21 = (bf16[256,256]{1,0:T(8,128)(2,1)S(1)}, bf16[256,256]{1,0:T(8,128)(2,1)S(1)}, u32[]{:S(2)}, u32[]{:S(2)}) collective-permute-start(bf16[256,256]{1,0:T(8,128)(2,1)S(1)} %convert_element_type.239), channel_id=1, source_target_pairs={{0,3},{1,0},{2,1},{3,2},{4,7},{5,4},{6,5},{7,6},{8,11},{9,8},{10,9... | collective-permute-start | bytes 393224 | tf_op jit(solution)/shard_map/ppermute | solution.py:281
  411.7 27.5 %collective-permute-start.14 = (bf16[256,640]{1,0:T(8,128)(2,1)}, bf16[256,640]{1,0:T(8,128)(2,1)S(1)}, u32[]{:S(2)}, u32[]{:S(2)}) collective-permute-start(bf16[256,640]{1,0:T(8,128)(2,1)} %add_convert_fusion.2), channel_id=1, source_target_pairs={{0,0},{1,4},{2,8},{3,12},{4,1},{5,5},{6,9},{7,13},{8,2},{9,6},{10,... | collective-permute-start | bytes 983048 | tf_op jit(solution)/shard_map/ppermute | solution.py:320
  419.3 26.0 %collective-permute-start.18 = (bf16[256,640]{1,0:T(8,128)(2,1)S(1)}, bf16[256,640]{1,0:T(8,128)(2,1)S(1)}, u32[]{:S(2)}, u32[]{:S(2)}) collective-permute-start(bf16[256,640]{1,0:T(8,128)(2,1)S(1)} %add_convert_fusion.1), channel_id=1, source_target_pairs={{0,0},{1,4},{2,8},{3,12},{4,1},{5,5},{6,9},{7,13},{8,2},{9,6},{10,... | collective-permute-start | bytes 983048 | tf_op jit(solution)/shard_map/ppermute | solution.py:320
  424.2 3.1 copy-start.1
  (23 other events, 30.5 us)
Sparse Core Ops, SparseCore 0:
  74.3 62.7 reduce-scatter.4
  140.0 68.4 reduce-scatter.2
  266.7 63.0 all-gather.4
  331.8 46.9 all-gather.6
